TPU v7x, 512 devices: a whole 4x8x8 slice. The times are simulated.
512 devices in a mesh: seq: 64 (over y, z), head: 8 (over x, core).
Axes of the slice: x: 4, y: 8, z: 8, core: 2. Of those that a mesh axis runs over, the one named last changes fastest.
Arguments:
- queries: bfloat16 [16384, 4096], P('seq', 'head'), may hold values from -120 to 120
- noisy_keys: bfloat16 [16384, 4096], P('seq', 'head'), may hold values from -120 to 120
- noisy_values: bfloat16 [16384, 4096], P('seq', 'head'), may hold values from -6 to 6
- clean_keys: bfloat16 [16384, 4096], P('seq', 'head'), may hold values from -120 to 120
- clean_values: bfloat16 [16384, 4096], P('seq', 'head'), may hold values from -6 to 6
- query_gain: float32 [4096], P('head'), may hold values from 0.25 to 1.75
- key_gain: float32 [4096], P('head'), may hold values from 0.25 to 1.75
- first_block: int32 [512], P('seq'), may hold values from 0 to 511, as said below
- loss_mask: int32 [16384], P('seq'), may hold values 0 or 1
- grad_output: bfloat16 [16384, 4096], P('seq', 'head'), may hold values from -6 to 6
Outputs:
- attended: bfloat16 [16384, 4096], P('seq', 'head')
- grad_queries: bfloat16 [16384, 4096], P('seq', 'head')
- grad_noisy_keys: bfloat16 [16384, 4096], P('seq', 'head')
- grad_noisy_values: bfloat16 [16384, 4096], P('seq', 'head')
- grad_clean_keys: bfloat16 [16384, 4096], P('seq', 'head')
- grad_clean_values: bfloat16 [16384, 4096], P('seq', 'head')
Inputs may be any that keep to these rules, and one draw needn't show every extreme that they name: first_block[b] is the first block of the document holding block b: it never falls, first_block[first_block[b]] = first_block[b], and b - first_block[b] < 48; at least one document holds exactly 48 blocks, and the last block is a document of its own.
All inputs are finite; a program needn't handle non-finite values. No bound on the sum of `loss_mask` on one device may be relied on, other than what follows from the above.
Results may differ from a plain program's by a relative error of at most 0.01055.
The roundings to bfloat16 on the way count: a program that leaves them out, or rounds other values in their place, can miss the bound.
Values may be sent and summed in bfloat16 or wider, within the bound.
No kernel may reach another device: no remote copies, remote signals or barrier semaphores. Data moves between devices by JAX's collectives and lax.ppermute only.
A program may use at most 64 MiB of HBM per device.

v0:
```python
from functools import partial

import jax
import jax.numpy as jnp
from jax import lax
from jax.sharding import PartitionSpec as P

HEAD_DIM = 128
BLOCK = 32
REACH = 6


EPS = 1e-06


def passed_along(shard, axis, by):
    count = lax.axis_size(axis)
    pairs = [(i, i + by) for i in range(count) if 0 <= i + by < count]
    return lax.ppermute(shard, axis, pairs)


def seen_mask(query_block, query_first, key_block):
    return (key_block[None, :] < query_block[:, None]) & (
        key_block[None, :] >= query_first[:, None]
    )


def tile_scores(query_heads, key_heads, softmax_scale):
    return (
        jnp.einsum("ihd,jhd->hij", query_heads, key_heads, preferred_element_type=jnp.float32)
        * softmax_scale
    )


def update_stats(running_max, running_total, query_heads, key_heads, visible, softmax_scale):
    scores = tile_scores(query_heads, key_heads, softmax_scale)
    masked = jnp.where(visible[None], scores, -jnp.inf)
    new_max = jnp.maximum(running_max, jnp.max(masked, axis=2))
    weights = jnp.where(visible[None], jnp.exp(scores - new_max[:, :, None]), 0.0)
    new_total = running_total * jnp.exp(running_max - new_max) + jnp.sum(weights, axis=2)
    return (new_max, new_total)


def tile_output(query_heads, key_heads, value_heads, visible, log_total, softmax_scale):
    scores = tile_scores(query_heads, key_heads, softmax_scale)
    weights = jnp.where(visible[None], jnp.exp(scores - log_total[:, :, None]), 0.0).astype(
        jnp.bfloat16
    )
    return jnp.einsum("hij,jhd->ihd", weights, value_heads, preferred_element_type=jnp.float32)


def tile_backward(
    query_heads, grad_heads, key_heads, value_heads, visible, log_total, delta, softmax_scale
):
    scores = tile_scores(query_heads, key_heads, softmax_scale)
    weights = jnp.where(visible[None], jnp.exp(scores - log_total[:, :, None]), 0.0)
    dweights = jnp.einsum(
        "ihd,jhd->hij", grad_heads, value_heads, preferred_element_type=jnp.float32
    )
    dscores = (weights * (dweights - delta[:, :, None])).astype(jnp.bfloat16)
    return (weights.astype(jnp.bfloat16), dscores)


def both_sides(
    query_heads, grad_heads, key_heads, value_heads, visible, log_total, delta, softmax_scale
):
    weight_bf, dscores = tile_backward(
        query_heads, grad_heads, key_heads, value_heads, visible, log_total, delta, softmax_scale
    )
    query_grad = jnp.einsum("hij,jhd->ihd", dscores, key_heads, preferred_element_type=jnp.float32)
    key_grad = jnp.einsum("hij,ihd->jhd", dscores, query_heads, preferred_element_type=jnp.float32)
    value_grad = jnp.einsum(
        "hij,ihd->jhd", weight_bf, grad_heads, preferred_element_type=jnp.float32
    )
    return (query_grad, key_grad.astype(jnp.bfloat16), value_grad.astype(jnp.bfloat16))


def unit_backward(values, inverse, term, inner, full_width):
    return (inverse[:, None] * term - values * (inverse**3 * inner / full_width)[:, None]).astype(
        jnp.bfloat16
    )


def local(
    queries,
    noisy_keys,
    noisy_values,
    clean_keys,
    clean_values,
    query_gain,
    key_gain,
    first_block,
    loss_mask,
    grad_output,
):
    row_count, local_width = queries.shape
    head_count = local_width // HEAD_DIM
    full_width = local_width * lax.axis_size("head")
    softmax_scale = HEAD_DIM ** (-0.5)
    shard_index = lax.axis_index("seq")
    block_count = row_count // BLOCK
    heads_shape = (row_count, head_count, HEAD_DIM)
    blocked_shape = (block_count, BLOCK, head_count, HEAD_DIM)
    query_raw = queries.astype(jnp.float32)
    noisy_raw = noisy_keys.astype(jnp.float32)
    clean_raw = clean_keys.astype(jnp.float32)
    totals = lax.psum(
        (
            jnp.sum(query_raw * query_raw, axis=1),
            jnp.sum(noisy_raw * noisy_raw, axis=1),
            jnp.sum(clean_raw * clean_raw, axis=1),
        ),
        "head",
    )
    query_inverse = lax.rsqrt(totals[0] / full_width + EPS)
    noisy_inverse = lax.rsqrt(totals[1] / full_width + EPS)
    clean_inverse = lax.rsqrt(totals[2] / full_width + EPS)
    query_unit = (query_raw * query_inverse[:, None] * query_gain[None, :]).astype(jnp.bfloat16)
    noisy_unit = (noisy_raw * noisy_inverse[:, None] * key_gain[None, :]).astype(jnp.bfloat16)
    clean_unit = (clean_raw * clean_inverse[:, None] * key_gain[None, :]).astype(jnp.bfloat16)
    local_block = jnp.arange(row_count, dtype=jnp.int32) // BLOCK
    row_block = shard_index * block_count + local_block
    row_first = jnp.repeat(first_block, BLOCK)
    query_heads = query_unit.reshape(heads_shape)
    query_blocked = query_unit.reshape(blocked_shape)
    noisy_blocked = noisy_unit.reshape(blocked_shape)
    value_blocked = noisy_values.reshape(blocked_shape)
    pieces = [(clean_unit, clean_values)]
    for distance in range(1, REACH + 1):
        pieces.append(passed_along((pieces[-1][0], pieces[-1][1]), "seq", 1))
    piece_heads = [
        (piece[0].reshape(heads_shape), piece[1].reshape(heads_shape)) for piece in pieces
    ]
    visibles = [
        seen_mask(row_block, row_first, (shard_index - distance) * block_count + local_block)
        for distance in range(REACH + 1)
    ]
    own_scores = (
        jnp.einsum(
            "bihd,bjhd->bhij", query_blocked, noisy_blocked, preferred_element_type=jnp.float32
        )
        * softmax_scale
    )
    own_max = jnp.max(own_scores, axis=3)
    running_max = own_max.transpose(1, 0, 2).reshape(head_count, row_count)
    running_total = (
        jnp.sum(jnp.exp(own_scores - own_max[..., None]), axis=3)
        .transpose(1, 0, 2)
        .reshape(head_count, row_count)
    )
    for distance in range(REACH + 1):
        running_max, running_total = lax.cond(
            jnp.any(visibles[distance]),
            partial(
                update_stats,
                query_heads=query_heads,
                key_heads=piece_heads[distance][0],
                visible=visibles[distance],
                softmax_scale=softmax_scale,
            ),
            lambda running_max, running_total: (running_max, running_total),
            running_max,
            running_total,
        )
    log_total = running_max + jnp.log(running_total)
    log_blocked = log_total.reshape(head_count, block_count, BLOCK).transpose(1, 0, 2)
    own_weights = jnp.exp(own_scores - log_blocked[..., None])
    own_weight_bf = own_weights.astype(jnp.bfloat16)
    output = jnp.einsum(
        "bhij,bjhd->bihd", own_weight_bf, value_blocked, preferred_element_type=jnp.float32
    ).reshape(heads_shape)
    zero_heads = jnp.zeros(heads_shape, jnp.float32)
    zero_narrow = jnp.zeros(heads_shape, jnp.bfloat16)
    for distance in range(REACH + 1):
        output = output + lax.cond(
            jnp.any(visibles[distance]),
            partial(
                tile_output,
                query_heads,
                piece_heads[distance][0],
                piece_heads[distance][1],
                visibles[distance],
                log_total,
                softmax_scale,
            ),
            lambda: zero_heads,
        )
    attended = output.reshape(row_count, local_width).astype(jnp.bfloat16)
    grad_masked = grad_output * loss_mask[:, None].astype(jnp.bfloat16)
    delta = jnp.sum(
        (grad_masked.astype(jnp.float32) * attended.astype(jnp.float32)).reshape(heads_shape),
        axis=2,
    ).T
    grad_heads = grad_masked.reshape(heads_shape)
    grad_blocked = grad_masked.reshape(blocked_shape)
    delta_blocked = delta.reshape(head_count, block_count, BLOCK).transpose(1, 0, 2)
    own_dweights = jnp.einsum(
        "bihd,bjhd->bhij", grad_blocked, value_blocked, preferred_element_type=jnp.float32
    )
    own_dscores = (own_weights * (own_dweights - delta_blocked[..., None])).astype(jnp.bfloat16)
    query_grad = jnp.einsum(
        "bhij,bjhd->bihd", own_dscores, noisy_blocked, preferred_element_type=jnp.float32
    ).reshape(heads_shape)
    noisy_grad = jnp.einsum(
        "bhij,bihd->bjhd", own_dscores, query_blocked, preferred_element_type=jnp.float32
    ).reshape(heads_shape)
    noisy_value_grad = jnp.einsum(
        "bhij,bihd->bjhd", own_weight_bf, grad_blocked, preferred_element_type=jnp.float32
    ).reshape(heads_shape)
    clean_grad = zero_heads
    clean_value_grad = zero_heads
    for distance in range(REACH + 1):
        contrib = lax.cond(
            jnp.any(visibles[distance]),
            partial(
                both_sides,
                query_heads,
                grad_heads,
                piece_heads[distance][0],
                piece_heads[distance][1],
                visibles[distance],
                log_total,
                delta,
                softmax_scale,
            ),
            lambda: (zero_heads, zero_narrow, zero_narrow),
        )
        query_grad = query_grad + contrib[0]
        if distance == 0:
            returned = (contrib[1], contrib[2])
        else:
            returned = passed_along((contrib[1], contrib[2]), "seq", -distance)
        clean_grad = clean_grad + returned[0].astype(jnp.float32)
        clean_value_grad = clean_value_grad + returned[1].astype(jnp.float32)
    query_term = query_gain[None, :] * (query_grad * softmax_scale).reshape(row_count, local_width)
    noisy_term = key_gain[None, :] * (noisy_grad * softmax_scale).reshape(row_count, local_width)
    clean_term = key_gain[None, :] * (clean_grad * softmax_scale).reshape(row_count, local_width)
    inner = lax.psum(
        (
            jnp.sum(query_term * query_raw, axis=1),
            jnp.sum(noisy_term * noisy_raw, axis=1),
            jnp.sum(clean_term * clean_raw, axis=1),
        ),
        "head",
    )
    grad_queries = unit_backward(query_raw, query_inverse, query_term, inner[0], full_width)
    grad_noisy_keys = unit_backward(noisy_raw, noisy_inverse, noisy_term, inner[1], full_width)
    grad_clean_keys = unit_backward(clean_raw, clean_inverse, clean_term, inner[2], full_width)
    grad_noisy_values = noisy_value_grad.reshape(row_count, local_width).astype(jnp.bfloat16)
    grad_clean_values = clean_value_grad.reshape(row_count, local_width).astype(jnp.bfloat16)
    return (
        attended,
        grad_queries,
        grad_noisy_keys,
        grad_noisy_values,
        grad_clean_keys,
        grad_clean_values,
    )


def solution(mesh):
    in_specs = (
        P("seq", "head"),
        P("seq", "head"),
        P("seq", "head"),
        P("seq", "head"),
        P("seq", "head"),
        P("head"),
        P("head"),
        P("seq"),
        P("seq"),
        P("seq", "head"),
    )
    out_specs = (
        P("seq", "head"),
        P("seq", "head"),
        P("seq", "head"),
        P("seq", "head"),
        P("seq", "head"),
        P("seq", "head"),
    )
    return jax.shard_map(local, mesh=mesh, in_specs=in_specs, out_specs=out_specs, check_vma=False)
```

profile of v0, /device:TPU:142, one launch (start us, length us, event | category | flops | bytes accessed | tf_op | source)
XLA Modules:
  0.0 281.0 jit_solution(5707743230000674774)
XLA Ops:
  2.9 10.5 %all-reduce.1 = (f32[256]{0:T(256)S(1)}, f32[256]{0:T(256)S(1)}, f32[256]{0:T(256)S(1)}) all-reduce(f32[256]{0:T(256)S(1)} %fusion.180, f32[256]{0:T(256)S(1)} %fusion.192, f32[256]{0:T(256)S(1)} %fusion.186), channel_id=1, replica_groups=mesh['seq'=64,'head'=8] {'head'}, use_global_device_ids=true, to_apply=%region_1.0 | all-reduce | flops 768 | bytes 6144 | tf_op jit(solution)/shard_map/psum | solution.py:107
  14.3 4.3 %collective-permute-start = (bf16[256,512]{1,0:T(8,128)(2,1)S(1)}, bf16[256,512]{1,0:T(8,128)(2,1)S(1)}, u32[]{:S(2)}, u32[]{:S(2)}) collective-permute-start(bf16[256,512]{1,0:T(8,128)(2,1)S(1)} %get-tuple-element.1239), channel_id=1, source_target_pairs={{0,8},{8,16},{16,24},{24,32},{32,40},{40,48},{48,56},{56,64},{64,7... | collective-permute-start | bytes 786440 | tf_op jit(solution)/shard_map/ppermute | solution.py:19
  18.7 5.5 %collective-permute-start.6 = (bf16[256,512]{0,1:T(8,128)(2,1)S(1)}, bf16[256,512]{0,1:T(8,128)(2,1)S(1)}, u32[]{:S(2)}, u32[]{:S(2)}) collective-permute-start(bf16[256,512]{0,1:T(8,128)(2,1)S(1)} %copy.569), channel_id=1, source_target_pairs={{0,8},{8,16},{16,24},{24,32},{32,40},{40,48},{48,56},{56,64},{64,7... | collective-permute-start | bytes 786440 | tf_op jit(solution)/shard_map/ppermute | solution.py:19
  25.2 5.4 %collective-permute-start.1 = (bf16[256,512]{1,0:T(8,128)(2,1)S(1)}, bf16[256,512]{1,0:T(8,128)(2,1)S(1)}, u32[]{:S(2)}, u32[]{:S(2)}) collective-permute-start(bf16[256,512]{1,0:T(8,128)(2,1)S(1)} %collective-permute-done), channel_id=1, source_target_pairs={{0,8},{8,16},{16,24},{24,32},{32,40},{40,48},{48,56},{56,64},{64,7... | collective-permute-start | bytes 786440 | tf_op jit(solution)/shard_map/ppermute | solution.py:19
  30.9 5.3 %collective-permute-start.7 = (bf16[256,512]{0,1:T(8,128)(2,1)S(1)}, bf16[256,512]{0,1:T(8,128)(2,1)S(1)}, u32[]{:S(2)}, u32[]{:S(2)}) collective-permute-start(bf16[256,512]{0,1:T(8,128)(2,1)S(1)} %collective-permute-done.6), channel_id=1, source_target_pairs={{0,8},{8,16},{16,24},{24,32},{32,40},{40,48},{48,56},{56,64},{64,7... | collective-permute-start | bytes 786440 | tf_op jit(solution)/shard_map/ppermute | solution.py:19
  36.9 5.8 %collective-permute-start.2 = (bf16[256,512]{1,0:T(8,128)(2,1)S(1)}, bf16[256,512]{1,0:T(8,128)(2,1)S(1)}, u32[]{:S(2)}, u32[]{:S(2)}) collective-permute-start(bf16[256,512]{1,0:T(8,128)(2,1)S(1)} %collective-permute-done.1), channel_id=1, source_target_pairs={{0,8},{8,16},{16,24},{24,32},{32,40},{40,48},{48,56},{56,64},{64,7... | collective-permute-start | bytes 786440 | tf_op jit(solution)/shard_map/ppermute | solution.py:19
  42.8 5.6 %collective-permute-start.8 = (bf16[256,512]{0,1:T(8,128)(2,1)S(1)}, bf16[256,512]{0,1:T(8,128)(2,1)S(1)}, u32[]{:S(2)}, u32[]{:S(2)}) collective-permute-start(bf16[256,512]{0,1:T(8,128)(2,1)S(1)} %collective-permute-done.7), channel_id=1, source_target_pairs={{0,8},{8,16},{16,24},{24,32},{32,40},{40,48},{48,56},{56,64},{64,7... | collective-permute-start | bytes 786440 | tf_op jit(solution)/shard_map/ppermute | solution.py:19
  48.5 5.4 %collective-permute-start.3 = (bf16[256,512]{1,0:T(8,128)(2,1)S(1)}, bf16[256,512]{1,0:T(8,128)(2,1)S(1)}, u32[]{:S(2)}, u32[]{:S(2)}) collective-permute-start(bf16[256,512]{1,0:T(8,128)(2,1)S(1)} %collective-permute-done.2), channel_id=1, source_target_pairs={{0,8},{8,16},{16,24},{24,32},{32,40},{40,48},{48,56},{56,64},{64,7... | collective-permute-start | bytes 786440 | tf_op jit(solution)/shard_map/ppermute | solution.py:19
  54.8 5.6 %collective-permute-start.9 = (bf16[256,512]{0,1:T(8,128)(2,1)S(1)}, bf16[256,512]{0,1:T(8,128)(2,1)}, u32[]{:S(2)}, u32[]{:S(2)}) collective-permute-start(bf16[256,512]{0,1:T(8,128)(2,1)S(1)} %collective-permute-done.8), channel_id=1, source_target_pairs={{0,8},{8,16},{16,24},{24,32},{32,40},{40,48},{48,56},{56,64},{64,7... | collective-permute-start | bytes 786440 | tf_op jit(solution)/shard_map/ppermute | solution.py:19
  60.6 5.5 %collective-permute-start.4 = (bf16[256,512]{1,0:T(8,128)(2,1)S(1)}, bf16[256,512]{1,0:T(8,128)(2,1)}, u32[]{:S(2)}, u32[]{:S(2)}) collective-permute-start(bf16[256,512]{1,0:T(8,128)(2,1)S(1)} %collective-permute-done.3), channel_id=1, source_target_pairs={{0,8},{8,16},{16,24},{24,32},{32,40},{40,48},{48,56},{56,64},{64,7... | collective-permute-start | bytes 786440 | tf_op jit(solution)/shard_map/ppermute | solution.py:19
  68.7 5.3 %collective-permute-start.10 = (bf16[256,512]{0,1:T(8,128)(2,1)}, bf16[256,512]{0,1:T(8,128)(2,1)}, u32[]{:S(2)}, u32[]{:S(2)}) collective-permute-start(bf16[256,512]{0,1:T(8,128)(2,1)} %collective-permute-done.9), channel_id=1, source_target_pairs={{0,8},{8,16},{16,24},{24,32},{32,40},{40,48},{48,56},{56,64},{64,7... | collective-permute-start | bytes 786440 | tf_op jit(solution)/shard_map/ppermute | solution.py:19
  74.1 3.4 %collective-permute-start.5 = (bf16[256,512]{1,0:T(8,128)(2,1)}, bf16[256,512]{1,0:T(8,128)(2,1)}, u32[]{:S(2)}, u32[]{:S(2)}) collective-permute-start(bf16[256,512]{1,0:T(8,128)(2,1)} %collective-permute-done.4), channel_id=1, source_target_pairs={{0,8},{8,16},{16,24},{24,32},{32,40},{40,48},{48,56},{56,64},{64,7... | collective-permute-start | bytes 786440 | tf_op jit(solution)/shard_map/ppermute | solution.py:19
  96.9 7.4 %collective-permute-start.11 = (bf16[256,512]{0,1:T(8,128)(2,1)}, bf16[256,512]{0,1:T(8,128)(2,1)}, u32[]{:S(2)}, u32[]{:S(2)}) collective-permute-start(bf16[256,512]{0,1:T(8,128)(2,1)} %collective-permute-done.10), channel_id=1, source_target_pairs={{0,8},{8,16},{16,24},{24,32},{32,40},{40,48},{48,56},{56,64},{64,7... | collective-permute-start | bytes 786440 | tf_op jit(solution)/shard_map/ppermute | solution.py:19
  110.9 2.4 conditional.30
  110.9 2.4 fusion.40
  115.5 2.4 conditional.31
  115.5 2.4 fusion.54
  126.2 5.1 %conditional.36 = (f32[256,4,128]{2,0,1:T(8,128)S(1)}, bf16[256,4,128]{2,0,1:T(8,128)(2,1)}, bf16[256,4,128]{2,0,1:T(8,128)(2,1)}) conditional(s32[]{:T(128)} %convert_element_type.304, () %tuple.187, (pred[256,256]{1,0:T(8,128)(4,1)S(1)}, bf16[256,4,128]{0,2,1:T(8,128)(2,1)S(1)}, bf16[256,4,128]{2,1,0:T(4,128)(2,1)}, f32[4,256]{1,0:T(4,128)S(1)}, ...), branch_computations={%region_60.61_spmd, %region_61.62_spmd} | conditional | flops 337641472 | bytes 8724532 | solution.py:213
  133.4 5.2 %conditional.37 = (f32[256,4,128]{2,0,1:T(8,128)S(1)}, bf16[256,4,128]{2,0,1:T(8,128)(2,1)}, bf16[256,4,128]{2,0,1:T(8,128)(2,1)}) conditional(s32[]{:T(128)} %convert_element_type.303, () %tuple.189, (pred[256,256]{1,0:T(8,128)(4,1)S(1)}, bf16[256,4,128]{0,2,1:T(8,128)(2,1)S(1)}, bf16[256,4,128]{2,1,0:T(4,128)(2,1)}, f32[4,256]{1,0:T(4,128)S(1)}, ...), branch_computations={%region_62.63_spmd, %region_63.64_spmd} | conditional | flops 337641472 | bytes 8724532 | solution.py:213
  140.7 5.2 %conditional.38 = (f32[256,4,128]{2,0,1:T(8,128)S(1)}, bf16[256,4,128]{2,0,1:T(8,128)(2,1)}, bf16[256,4,128]{2,0,1:T(8,128)(2,1)}) conditional(s32[]{:T(128)} %convert_element_type.302, () %tuple.191, (pred[256,256]{1,0:T(8,128)(4,1)S(1)}, bf16[256,4,128]{0,2,1:T(8,128)(2,1)S(1)}, bf16[256,4,128]{2,1,0:T(4,128)(2,1)}, f32[4,256]{1,0:T(4,128)S(1)}, ...), branch_computations={%region_64.65_spmd, %region_65.66_spmd} | conditional | flops 337641472 | bytes 8724532 | solution.py:213
  145.9 4.0 %collective-permute-start.14 = (bf16[256,4,128]{2,0,1:T(8,128)(2,1)}, bf16[256,4,128]{2,0,1:T(8,128)(2,1)}, u32[]{:S(2)}, u32[]{:S(2)}) collective-permute-start(bf16[256,4,128]{2,0,1:T(8,128)(2,1)} %get-tuple-element.483), channel_id=1, source_target_pairs={{24,0},{32,8},{40,16},{48,24},{56,32},{64,40},{72,48},{80,56},{88,... | collective-permute-start | bytes 786440 | tf_op jit(solution)/shard_map/ppermute | solution.py:19
  150.0 6.1 %conditional.39 = (f32[256,4,128]{2,0,1:T(8,128)S(1)}, bf16[256,4,128]{2,0,1:T(8,128)(2,1)}, bf16[256,4,128]{2,0,1:T(8,128)(2,1)}) conditional(s32[]{:T(128)} %convert_element_type.301, () %tuple.193, (pred[256,256]{1,0:T(8,128)(4,1)S(1)}, bf16[256,4,128]{0,2,1:T(8,128)(2,1)S(1)}, bf16[256,4,128]{2,1,0:T(4,128)(2,1)}, f32[4,256]{1,0:T(4,128)S(1)}, ...), branch_computations={%region_66.67_spmd, %region_67.68_spmd} | conditional | flops 337641472 | bytes 7675928 | solution.py:213
  156.0 7.0 %collective-permute-start.15 = (bf16[256,4,128]{2,0,1:T(8,128)(2,1)}, bf16[256,4,128]{2,0,1:T(8,128)(2,1)}, u32[]{:S(2)}, u32[]{:S(2)}) collective-permute-start(bf16[256,4,128]{2,0,1:T(8,128)(2,1)} %get-tuple-element.484), channel_id=1, source_target_pairs={{32,0},{40,8},{48,16},{56,24},{64,32},{72,40},{80,48},{88,56},{96,... | collective-permute-start | bytes 786440 | tf_op jit(solution)/shard_map/ppermute | solution.py:19
  165.3 3.6 %collective-permute-start.16 = (bf16[256,4,128]{2,0,1:T(8,128)(2,1)}, bf16[256,4,128]{2,0,1:T(8,128)(2,1)}, u32[]{:S(2)}, u32[]{:S(2)}) collective-permute-start(bf16[256,4,128]{2,0,1:T(8,128)(2,1)} %get-tuple-element.485), channel_id=1, source_target_pairs={{40,0},{48,8},{56,16},{64,24},{72,32},{80,40},{88,48},{96,56},{104... | collective-permute-start | bytes 786440 | tf_op jit(solution)/shard_map/ppermute | solution.py:19
  175.0 3.4 %fusion.204 = f32[256,4,128]{2,0,1:T(8,128)} fusion(f32[256,4,128]{2,0,1:T(8,128)} %get-tuple-element.479, f32[256,4,128]{2,0,1:T(8,128)} %copy-done.6, f32[256,4,128]{2,0,1:T(8,128)} %copy-done.5, f32[256,4,128]{2,0,1:T(8,128)} %copy-done.4, f32[256,4,128]{2,0,1:T(8,128)} %copy-done.3, f32[256,4,128]{2,0,1:T(8,128)} %copy-done.2, ...), kind=kLoop, calls=%fused_computation.288 | loop fusion | flops 1048576 | bytes 4718592 | tf_op jit(solution)/shard_map/mul | solution.py:235
  188.4 5.3 %collective-permute-start.19 = (bf16[256,4,128]{2,0,1:T(8,128)(2,1)}, bf16[256,4,128]{2,0,1:T(8,128)(2,1)S(1)}, u32[]{:S(2)}, u32[]{:S(2)}) collective-permute-start(bf16[256,4,128]{2,0,1:T(8,128)(2,1)} %get-tuple-element.489), channel_id=1, source_target_pairs={{16,0},{24,8},{32,16},{40,24},{48,32},{56,40},{64,48},{72,56},{80,... | collective-permute-start | bytes 786440 | tf_op jit(solution)/shard_map/ppermute | solution.py:19
  193.7 4.4 %collective-permute-start.20 = (bf16[256,4,128]{2,0,1:T(8,128)(2,1)}, bf16[256,4,128]{2,0,1:T(8,128)(2,1)}, u32[]{:S(2)}, u32[]{:S(2)}) collective-permute-start(bf16[256,4,128]{2,0,1:T(8,128)(2,1)} %get-tuple-element.490), channel_id=1, source_target_pairs={{24,0},{32,8},{40,16},{48,24},{56,32},{64,40},{72,48},{80,56},{88,... | collective-permute-start | bytes 786440 | tf_op jit(solution)/shard_map/ppermute | solution.py:19
  198.2 4.6 %collective-permute-done.16 = bf16[256,4,128]{2,0,1:T(8,128)(2,1)} collective-permute-done((bf16[256,4,128]{2,0,1:T(8,128)(2,1)}, bf16[256,4,128]{2,0,1:T(8,128)(2,1)}, u32[]{:S(2)}, u32[]{:S(2)}) %collective-permute-start.16) | collective-permute-done | bytes 262176 | tf_op jit(solution)/shard_map/ppermute | solution.py:19
  204.6 3.6 %collective-permute-done.17 = bf16[256,4,128]{2,0,1:T(8,128)(2,1)S(1)} collective-permute-done((bf16[256,4,128]{2,0,1:T(8,128)(2,1)S(1)}, bf16[256,4,128]{2,0,1:T(8,128)(2,1)S(1)}, u32[]{:S(2)}, u32[]{:S(2)}) %collective-permute-start.17) | collective-permute-done | bytes 262176 | tf_op jit(solution)/shard_map/ppermute | solution.py:19
  212.2 11.5 %all-reduce = (f32[256]{0:T(256)S(1)}, f32[256]{0:T(256)S(1)}, f32[256]{0:T(256)S(1)}) all-reduce(f32[256]{0:T(256)S(1)} %fusion.183, f32[256]{0:T(256)S(1)} %fusion.189, f32[256]{0:T(256)S(1)} %fusion.195), channel_id=1, replica_groups=mesh['seq'=64,'head'=8] {'head'}, use_global_device_ids=true, to_apply=%region_73.74 | all-reduce | flops 768 | bytes 6144 | tf_op jit(solution)/shard_map/psum | solution.py:238
  225.6 6.7 %collective-permute-start.23 = (bf16[256,4,128]{2,0,1:T(8,128)(2,1)S(1)}, bf16[256,4,128]{2,0,1:T(8,128)(2,1)S(1)}, u32[]{:S(2)}, u32[]{:S(2)}) collective-permute-start(bf16[256,4,128]{2,0,1:T(8,128)(2,1)S(1)} %copy-done.32), channel_id=1, source_target_pairs={{48,0},{56,8},{64,16},{72,24},{80,32},{88,40},{96,48},{104,56},{11... | collective-permute-start | bytes 786440 | tf_op jit(solution)/shard_map/ppermute | solution.py:19
  234.3 44.7 %collective-permute-done.23 = bf16[256,4,128]{2,0,1:T(8,128)(2,1)S(1)} collective-permute-done((bf16[256,4,128]{2,0,1:T(8,128)(2,1)S(1)}, bf16[256,4,128]{2,0,1:T(8,128)(2,1)S(1)}, u32[]{:S(2)}, u32[]{:S(2)}) %collective-permute-start.23) | collective-permute-done | bytes 262176 | tf_op jit(solution)/shard_map/ppermute | solution.py:19
  (294 shorter events, 116.3 us)
Async XLA Ops:
  14.3 10.9 %collective-permute-start = (bf16[256,512]{1,0:T(8,128)(2,1)S(1)}, bf16[256,512]{1,0:T(8,128)(2,1)S(1)}, u32[]{:S(2)}, u32[]{:S(2)}) collective-permute-start(bf16[256,512]{1,0:T(8,128)(2,1)S(1)} %get-tuple-element.1239), channel_id=1, source_target_pairs={{0,8},{8,16},{16,24},{24,32},{32,40},{40,48},{48,56},{56,64},{64,7... | collective-permute-start | bytes 786440 | tf_op jit(solution)/shard_map/ppermute | solution.py:19
  18.7 36.1 %copy-start.15 = (bf16[256,512]{0,1:T(8,128)(2,1)}, bf16[256,512]{0,1:T(8,128)(2,1)S(1)}, u32[]{:S(2)}) copy-start(bf16[256,512]{0,1:T(8,128)(2,1)S(1)} %copy.569) | copy-start | bytes 786436
  18.7 12.1 %collective-permute-start.6 = (bf16[256,512]{0,1:T(8,128)(2,1)S(1)}, bf16[256,512]{0,1:T(8,128)(2,1)S(1)}, u32[]{:S(2)}, u32[]{:S(2)}) collective-permute-start(bf16[256,512]{0,1:T(8,128)(2,1)S(1)} %copy.569), channel_id=1, source_target_pairs={{0,8},{8,16},{16,24},{24,32},{32,40},{40,48},{48,56},{56,64},{64,7... | collective-permute-start | bytes 786440 | tf_op jit(solution)/shard_map/ppermute | solution.py:19
  25.2 11.7 %collective-permute-start.1 = (bf16[256,512]{1,0:T(8,128)(2,1)S(1)}, bf16[256,512]{1,0:T(8,128)(2,1)S(1)}, u32[]{:S(2)}, u32[]{:S(2)}) collective-permute-start(bf16[256,512]{1,0:T(8,128)(2,1)S(1)} %collective-permute-done), channel_id=1, source_target_pairs={{0,8},{8,16},{16,24},{24,32},{32,40},{40,48},{48,56},{56,64},{64,7... | collective-permute-start | bytes 786440 | tf_op jit(solution)/shard_map/ppermute | solution.py:19
  30.9 23.1 %copy-start.47 = (bf16[256,512]{0,1:T(8,128)(2,1)}, bf16[256,512]{0,1:T(8,128)(2,1)S(1)}, u32[]{:S(2)}) copy-start(bf16[256,512]{0,1:T(8,128)(2,1)S(1)} %collective-permute-done.6) | copy-start | bytes 786436
  30.9 11.9 %collective-permute-start.7 = (bf16[256,512]{0,1:T(8,128)(2,1)S(1)}, bf16[256,512]{0,1:T(8,128)(2,1)S(1)}, u32[]{:S(2)}, u32[]{:S(2)}) collective-permute-start(bf16[256,512]{0,1:T(8,128)(2,1)S(1)} %collective-permute-done.6), channel_id=1, source_target_pairs={{0,8},{8,16},{16,24},{24,32},{32,40},{40,48},{48,56},{56,64},{64,7... | collective-permute-start | bytes 786440 | tf_op jit(solution)/shard_map/ppermute | solution.py:19
  36.9 17.9 %copy-start.21 = (bf16[256,512]{1,0:T(8,128)(2,1)}, bf16[256,512]{1,0:T(8,128)(2,1)S(1)}, u32[]{:S(2)}) copy-start(bf16[256,512]{1,0:T(8,128)(2,1)S(1)} %collective-permute-done.1) | copy-start | bytes 786436
  36.9 11.6 %collective-permute-start.2 = (bf16[256,512]{1,0:T(8,128)(2,1)S(1)}, bf16[256,512]{1,0:T(8,128)(2,1)S(1)}, u32[]{:S(2)}, u32[]{:S(2)}) collective-permute-start(bf16[256,512]{1,0:T(8,128)(2,1)S(1)} %collective-permute-done.1), channel_id=1, source_target_pairs={{0,8},{8,16},{16,24},{24,32},{32,40},{40,48},{48,56},{56,64},{64,7... | collective-permute-start | bytes 786440 | tf_op jit(solution)/shard_map/ppermute | solution.py:19
  42.8 25.5 %copy-start.51 = (bf16[256,512]{0,1:T(8,128)(2,1)}, bf16[256,512]{0,1:T(8,128)(2,1)S(1)}, u32[]{:S(2)}) copy-start(bf16[256,512]{0,1:T(8,128)(2,1)S(1)} %collective-permute-done.7) | copy-start | bytes 786436
  42.8 12.0 %collective-permute-start.8 = (bf16[256,512]{0,1:T(8,128)(2,1)S(1)}, bf16[256,512]{0,1:T(8,128)(2,1)S(1)}, u32[]{:S(2)}, u32[]{:S(2)}) collective-permute-start(bf16[256,512]{0,1:T(8,128)(2,1)S(1)} %collective-permute-done.7), channel_id=1, source_target_pairs={{0,8},{8,16},{16,24},{24,32},{32,40},{40,48},{48,56},{56,64},{64,7... | collective-permute-start | bytes 786440 | tf_op jit(solution)/shard_map/ppermute | solution.py:19
  48.5 19.6 %copy-start.25 = (bf16[256,512]{1,0:T(8,128)(2,1)}, bf16[256,512]{1,0:T(8,128)(2,1)S(1)}, u32[]{:S(2)}) copy-start(bf16[256,512]{1,0:T(8,128)(2,1)S(1)} %collective-permute-done.2) | copy-start | bytes 786436
  48.5 12.1 %collective-permute-start.3 = (bf16[256,512]{1,0:T(8,128)(2,1)S(1)}, bf16[256,512]{1,0:T(8,128)(2,1)S(1)}, u32[]{:S(2)}, u32[]{:S(2)}) collective-permute-start(bf16[256,512]{1,0:T(8,128)(2,1)S(1)} %collective-permute-done.2), channel_id=1, source_target_pairs={{0,8},{8,16},{16,24},{24,32},{32,40},{40,48},{48,56},{56,64},{64,7... | collective-permute-start | bytes 786440 | tf_op jit(solution)/shard_map/ppermute | solution.py:19
  54.8 13.9 %collective-permute-start.9 = (bf16[256,512]{0,1:T(8,128)(2,1)S(1)}, bf16[256,512]{0,1:T(8,128)(2,1)}, u32[]{:S(2)}, u32[]{:S(2)}) collective-permute-start(bf16[256,512]{0,1:T(8,128)(2,1)S(1)} %collective-permute-done.8), channel_id=1, source_target_pairs={{0,8},{8,16},{16,24},{24,32},{32,40},{40,48},{48,56},{56,64},{64,7... | collective-permute-start | bytes 786440 | tf_op jit(solution)/shard_map/ppermute | solution.py:19
  60.6 13.5 %collective-permute-start.4 = (bf16[256,512]{1,0:T(8,128)(2,1)S(1)}, bf16[256,512]{1,0:T(8,128)(2,1)}, u32[]{:S(2)}, u32[]{:S(2)}) collective-permute-start(bf16[256,512]{1,0:T(8,128)(2,1)S(1)} %collective-permute-done.3), channel_id=1, source_target_pairs={{0,8},{8,16},{16,24},{24,32},{32,40},{40,48},{48,56},{56,64},{64,7... | collective-permute-start | bytes 786440 | tf_op jit(solution)/shard_map/ppermute | solution.py:19
  68.7 28.2 %collective-permute-start.10 = (bf16[256,512]{0,1:T(8,128)(2,1)}, bf16[256,512]{0,1:T(8,128)(2,1)}, u32[]{:S(2)}, u32[]{:S(2)}) collective-permute-start(bf16[256,512]{0,1:T(8,128)(2,1)} %collective-permute-done.9), channel_id=1, source_target_pairs={{0,8},{8,16},{16,24},{24,32},{32,40},{40,48},{48,56},{56,64},{64,7... | collective-permute-start | bytes 786440 | tf_op jit(solution)/shard_map/ppermute | solution.py:19
  74.1 30.3 %collective-permute-start.5 = (bf16[256,512]{1,0:T(8,128)(2,1)}, bf16[256,512]{1,0:T(8,128)(2,1)}, u32[]{:S(2)}, u32[]{:S(2)}) collective-permute-start(bf16[256,512]{1,0:T(8,128)(2,1)} %collective-permute-done.4), channel_id=1, source_target_pairs={{0,8},{8,16},{16,24},{24,32},{32,40},{40,48},{48,56},{56,64},{64,7... | collective-permute-start | bytes 786440 | tf_op jit(solution)/shard_map/ppermute | solution.py:19
  77.7 35.7 %copy-start.12 = (bf16[256,4,128]{2,1,0:T(4,128)(2,1)}, bf16[256,4,128]{2,1,0:T(4,128)(2,1)S(1)}, u32[]{:S(2)}) copy-start(bf16[256,4,128]{2,1,0:T(4,128)(2,1)S(1)} %reshape.223) | copy-start | bytes 786436
  96.9 11.6 %collective-permute-start.11 = (bf16[256,512]{0,1:T(8,128)(2,1)}, bf16[256,512]{0,1:T(8,128)(2,1)}, u32[]{:S(2)}, u32[]{:S(2)}) collective-permute-start(bf16[256,512]{0,1:T(8,128)(2,1)} %collective-permute-done.10), channel_id=1, source_target_pairs={{0,8},{8,16},{16,24},{24,32},{32,40},{40,48},{48,56},{56,64},{64,7... | collective-permute-start | bytes 786440 | tf_op jit(solution)/shard_map/ppermute | solution.py:19
  131.4 50.8 %collective-permute-start.12 = (bf16[256,4,128]{2,0,1:T(8,128)(2,1)}, bf16[256,4,128]{2,0,1:T(8,128)(2,1)}, u32[]{:S(2)}, u32[]{:S(2)}) collective-permute-start(bf16[256,4,128]{2,0,1:T(8,128)(2,1)} %get-tuple-element.481), channel_id=1, source_target_pairs={{8,0},{16,8},{24,16},{32,24},{40,32},{48,40},{56,48},{64,56},{72,6... | collective-permute-start | bytes 786440 | tf_op jit(solution)/shard_map/ppermute | solution.py:19
  138.6 47.9 %collective-permute-start.13 = (bf16[256,4,128]{2,0,1:T(8,128)(2,1)}, bf16[256,4,128]{2,0,1:T(8,128)(2,1)}, u32[]{:S(2)}, u32[]{:S(2)}) collective-permute-start(bf16[256,4,128]{2,0,1:T(8,128)(2,1)} %get-tuple-element.482), channel_id=1, source_target_pairs={{16,0},{24,8},{32,16},{40,24},{48,32},{56,40},{64,48},{72,56},{80,... | collective-permute-start | bytes 786440 | tf_op jit(solution)/shard_map/ppermute | solution.py:19
  145.9 42.5 %collective-permute-start.14 = (bf16[256,4,128]{2,0,1:T(8,128)(2,1)}, bf16[256,4,128]{2,0,1:T(8,128)(2,1)}, u32[]{:S(2)}, u32[]{:S(2)}) collective-permute-start(bf16[256,4,128]{2,0,1:T(8,128)(2,1)} %get-tuple-element.483), channel_id=1, source_target_pairs={{24,0},{32,8},{40,16},{48,24},{56,32},{64,40},{72,48},{80,56},{88,... | collective-permute-start | bytes 786440 | tf_op jit(solution)/shard_map/ppermute | solution.py:19
  156.0 37.7 %collective-permute-start.15 = (bf16[256,4,128]{2,0,1:T(8,128)(2,1)}, bf16[256,4,128]{2,0,1:T(8,128)(2,1)}, u32[]{:S(2)}, u32[]{:S(2)}) collective-permute-start(bf16[256,4,128]{2,0,1:T(8,128)(2,1)} %get-tuple-element.484), channel_id=1, source_target_pairs={{32,0},{40,8},{48,16},{56,24},{64,32},{72,40},{80,48},{88,56},{96,... | collective-permute-start | bytes 786440 | tf_op jit(solution)/shard_map/ppermute | solution.py:19
  165.3 37.4 %collective-permute-start.16 = (bf16[256,4,128]{2,0,1:T(8,128)(2,1)}, bf16[256,4,128]{2,0,1:T(8,128)(2,1)}, u32[]{:S(2)}, u32[]{:S(2)}) collective-permute-start(bf16[256,4,128]{2,0,1:T(8,128)(2,1)} %get-tuple-element.485), channel_id=1, source_target_pairs={{40,0},{48,8},{56,16},{64,24},{72,32},{80,40},{88,48},{96,56},{104... | collective-permute-start | bytes 786440 | tf_op jit(solution)/shard_map/ppermute | solution.py:19
  182.2 26.0 %collective-permute-start.17 = (bf16[256,4,128]{2,0,1:T(8,128)(2,1)S(1)}, bf16[256,4,128]{2,0,1:T(8,128)(2,1)S(1)}, u32[]{:S(2)}, u32[]{:S(2)}) collective-permute-start(bf16[256,4,128]{2,0,1:T(8,128)(2,1)S(1)} %copy-done.30), channel_id=1, source_target_pairs={{48,0},{56,8},{64,16},{72,24},{80,32},{88,40},{96,48},{104,56},{11... | collective-permute-start | bytes 786440 | tf_op jit(solution)/shard_map/ppermute | solution.py:19
  184.3 25.9 %copy-start.9 = (f32[256,4,128]{2,0,1:T(8,128)S(1)}, f32[256,4,128]{2,0,1:T(8,128)}, u32[]{:S(2)}) copy-start(f32[256,4,128]{2,0,1:T(8,128)} %copy-done.8) | copy-start | bytes 1572868
  186.5 38.3 %collective-permute-start.18 = (bf16[256,4,128]{2,0,1:T(8,128)(2,1)}, bf16[256,4,128]{2,0,1:T(8,128)(2,1)S(1)}, u32[]{:S(2)}, u32[]{:S(2)}) collective-permute-start(bf16[256,4,128]{2,0,1:T(8,128)(2,1)} %get-tuple-element.488), channel_id=1, source_target_pairs={{8,0},{16,8},{24,16},{32,24},{40,32},{48,40},{56,48},{64,56},{72,6... | collective-permute-start | bytes 786440 | tf_op jit(solution)/shard_map/ppermute | solution.py:19
  188.4 45.6 %collective-permute-start.19 = (bf16[256,4,128]{2,0,1:T(8,128)(2,1)}, bf16[256,4,128]{2,0,1:T(8,128)(2,1)S(1)}, u32[]{:S(2)}, u32[]{:S(2)}) collective-permute-start(bf16[256,4,128]{2,0,1:T(8,128)(2,1)} %get-tuple-element.489), channel_id=1, source_target_pairs={{16,0},{24,8},{32,16},{40,24},{48,32},{56,40},{64,48},{72,56},{80,... | collective-permute-start | bytes 786440 | tf_op jit(solution)/shard_map/ppermute | solution.py:19
  193.7 40.6 %collective-permute-start.20 = (bf16[256,4,128]{2,0,1:T(8,128)(2,1)}, bf16[256,4,128]{2,0,1:T(8,128)(2,1)}, u32[]{:S(2)}, u32[]{:S(2)}) collective-permute-start(bf16[256,4,128]{2,0,1:T(8,128)(2,1)} %get-tuple-element.490), channel_id=1, source_target_pairs={{24,0},{32,8},{40,16},{48,24},{56,32},{64,40},{72,48},{80,56},{88,... | collective-permute-start | bytes 786440 | tf_op jit(solution)/shard_map/ppermute | solution.py:19
  202.7 31.6 %collective-permute-start.21 = (bf16[256,4,128]{2,0,1:T(8,128)(2,1)}, bf16[256,4,128]{2,0,1:T(8,128)(2,1)}, u32[]{:S(2)}, u32[]{:S(2)}) collective-permute-start(bf16[256,4,128]{2,0,1:T(8,128)(2,1)} %get-tuple-element.491), channel_id=1, source_target_pairs={{32,0},{40,8},{48,16},{56,24},{64,32},{72,40},{80,48},{88,56},{96,... | collective-permute-start | bytes 786440 | tf_op jit(solution)/shard_map/ppermute | solution.py:19
  208.2 26.1 %collective-permute-start.22 = (bf16[256,4,128]{2,0,1:T(8,128)(2,1)}, bf16[256,4,128]{2,0,1:T(8,128)(2,1)}, u32[]{:S(2)}, u32[]{:S(2)}) collective-permute-start(bf16[256,4,128]{2,0,1:T(8,128)(2,1)} %get-tuple-element.492), channel_id=1, source_target_pairs={{40,0},{48,8},{56,16},{64,24},{72,32},{80,40},{88,48},{96,56},{104... | collective-permute-start | bytes 786440 | tf_op jit(solution)/shard_map/ppermute | solution.py:19
  225.6 53.4 %collective-permute-start.23 = (bf16[256,4,128]{2,0,1:T(8,128)(2,1)S(1)}, bf16[256,4,128]{2,0,1:T(8,128)(2,1)S(1)}, u32[]{:S(2)}, u32[]{:S(2)}) collective-permute-start(bf16[256,4,128]{2,0,1:T(8,128)(2,1)S(1)} %copy-done.32), channel_id=1, source_target_pairs={{48,0},{56,8},{64,16},{72,24},{80,32},{88,40},{96,48},{104,56},{11... | collective-permute-start | bytes 786440 | tf_op jit(solution)/shard_map/ppermute | solution.py:19
  233.1 45.9 %copy-start.11 = (f32[256,4,128]{2,0,1:T(8,128)S(1)}, f32[256,4,128]{2,0,1:T(8,128)}, u32[]{:S(2)}) copy-start(f32[256,4,128]{2,0,1:T(8,128)} %copy-done.10) | copy-start | bytes 1572868
  (49 other events, 143.3 us)
where the time goes:
time: 284 us; the launch traced here: 281 us
  starting transfers between devices  107 us (38%)
  waiting for transfers between devices  59.3 us (21%)
  matrix products  41.8 us (15%)
  local copies, waits for them, and re-layouts  28.7 us (10%)
  blocking collectives  22.1 us (8%)
  other arithmetic  15.6 us (5%)
  between operations  5.98 us (2%)
    ppermute x24, starting transfers between devices, passed_along(): return lax.ppermute(shard, axis, pairs)  107 us
    ppermute x24, waiting for transfers between devices, passed_along(): return lax.ppermute(shard, axis, pairs)  59.3 us
    unnamed x114, local copies, waits for them, and re-layouts  13 us
    dot_general x5, matrix products, tile_output(): jnp.einsum('hij,jhd->ihd', weights, value_heads, preferred_element_type=j...  11.8 us
    psum x1, blocking collectives, local(): lax.psum((jnp.sum(query_term * query_raw, axis=1), jnp.sum(noisy_term * n...  11.5 us
    dot_general x10, matrix products, tile_scores(): jnp.einsum('ihd,jhd->hij', query_heads, key_heads, preferred_element_type...  11.4 us
    psum x1, blocking collectives, local(): lax.psum((jnp.sum(query_raw * query_raw, axis=1), jnp.sum(noisy_raw * noi...  10.5 us
    reshape x7, local copies, waits for them, and re-layouts, local(): piece[0].reshape(heads_shape)  6.6 us
  transfers between devices with their start and end apart: 24, of which 11 were waited for; matrix products, arithmetic and copies ran while one was open for 19% of the time, Pallas kernels for 0%

commit v1 on v0

v1 whole, which is shorter than its diff:
```python
from functools import partial

import jax
import jax.numpy as jnp
from jax import lax
from jax.experimental import pallas as pl
from jax.experimental.pallas import tpu as pltpu
from jax.sharding import PartitionSpec as P

HEAD_DIM = 128
BLOCK = 32
RING = 8
EPS = 1e-06
LOG2E = 1.4426950408889634
HIDDEN = -1e30
SCALE = HEAD_DIM ** (-0.5)
F32 = jnp.float32
BF16 = jnp.bfloat16

OWN, FOURTH = (0, 0), (4, -4)
FIRST = [(1, -1), (-1, 1)]
SECOND = [(2, -2), (-2, 2)]
THIRD = [(3, -3), (-3, 3)]
NOISY = None


def shifted(shard, by):
    count = lax.axis_size("seq")
    return lax.ppermute(shard, "seq", [(i, (i + by) % count) for i in range(count)])


def ring_groups():
    count = lax.axis_size("seq")
    return [list(range(start, start + RING)) for start in range(0, count, RING)]


def ring_gather(shard):
    return lax.all_gather(shard, "seq", axis_index_groups=ring_groups(), tiled=True)


def ring_scatter(parts):
    return lax.psum_scatter(
        parts, "seq", scatter_dimension=0, axis_index_groups=ring_groups(), tiled=True
    )


def swapped(shard, first):
    pairs = []
    for start in range(0, lax.axis_size("seq"), RING):
        for left in range(first, RING, 2):
            one, other = start + left, start + (left + 1) % RING
            pairs += [(one, other), (other, one)]
    return lax.ppermute(shard, "seq", pairs)


def add_kernel(unread, *refs):
    left_ref, right_ref, out_ref = refs[unread:]
    out_ref[...] = left_ref[...] + right_ref[...]


def head_sum(values, before_last=()):
    count = lax.axis_size("head")
    if count & (count - 1):
        return lax.psum(values, "head")
    bit = 1
    while bit < count:
        other = lax.ppermute(values, "head", [(i, i ^ bit) for i in range(count)])
        if before_last and 4 * bit == count:
            (values,) = call(
                partial(add_kernel, len(before_last)),
                "add",
                [(values.shape, F32)],
                1024,
                values,
                other,
                unread=before_last,
            )
        else:
            values = values + other
        bit *= 2
    return values


def dot(left, right):
    return jnp.dot(left, right, preferred_element_type=F32)


def lanes(head):
    return slice(head * HEAD_DIM, (head + 1) * HEAD_DIM)


def stacked(blocks):
    return jnp.concatenate(blocks, axis=0)


def tile_place(where_ref, tile):
    if tile is NOISY:
        return RING, 0
    place = where_ref[0]
    far = jnp.where(where_ref[1] == 1, tile[1], tile[0])
    index = lax.rem(place + far + RING, RING)
    return index, jnp.where(index > place, 1, 0)


def value_rows(index, rows):
    return pl.ds(pl.multiple_of(index * rows, rows), rows)


def softmax_tile(keys, values, query_t, shift):
    raw = dot(keys, query_t) * (SCALE * LOG2E)
    scores = [
        raw[block * BLOCK : (block + 1) * BLOCK] + shift[block : block + 1]
        for block in range(shift.shape[0])
    ]
    top = scores[0]
    for block in scores[1:]:
        top = jnp.maximum(top, block)
    top = jnp.max(top, axis=0, keepdims=True)
    weights = [jnp.exp2(block - top) for block in scores]
    total = weights[0]
    for block in weights[1:]:
        total = total + block
    total = jnp.sum(total, axis=0, keepdims=True)
    acc = dot(values.T, stacked([w.astype(BF16) for w in weights]))
    return top, total, acc


def forward_kernel(
    tiles,
    where_ref,
    bias_ref,
    q_ref,
    q_next_ref,
    g_ref,
    g_next_ref,
    noisy_values_ref,
    values_ref,
    *refs,
):
    count = len(tiles)
    keys_refs = refs[:count]
    qt_ref, gt_ref, q_both, g_both, stat_ref, acc_ref = refs[count:]
    rows = bias_ref.shape[-1]
    heads = q_ref.shape[1] // HEAD_DIM
    for which, (q, g) in enumerate(((q_ref, g_ref), (q_next_ref, g_next_ref))):
        q_both[which], g_both[which] = q[...], g[...]
        for head in range(heads):
            part = lanes(head)
            qt_ref[which, part, :] = q[:, part].T
            gt_ref[which, part, :] = g[:, part].T
    for number, tile in enumerate(tiles):
        index, which = tile_place(where_ref, tile)
        for head in range(heads):
            part = lanes(head)
            if tile is NOISY:
                values = noisy_values_ref[:, part]
            else:
                values = values_ref[value_rows(index, rows), part]
            top, total, acc = softmax_tile(
                keys_refs[number][:, part], values, qt_ref[which, part, :], bias_ref[index]
            )
            stat_ref[2 * number, head : head + 1, :] = top
            stat_ref[2 * number + 1, head : head + 1, :] = total
            acc_ref[number, part, :] = acc


def forward_end_kernel(
    tiles, before, where_ref, bias_ref, qt_ref, gt_ref, stat_ref, acc_ref, values_ref, *refs
):
    count = len(tiles)
    keys_refs = refs[:count]
    own_stat, next_stat, own_acc, next_acc = refs[count:]
    rows = bias_ref.shape[-1]
    heads = values_ref.shape[1] // HEAD_DIM
    places = [tile_place(where_ref, tile) for tile in (*before, *tiles)]
    for head in range(heads):
        part = lanes(head)
        parts = [
            (
                stat_ref[2 * number, head : head + 1, :],
                stat_ref[2 * number + 1, head : head + 1, :],
                acc_ref[number, part, :],
            )
            for number in range(len(before))
        ]
        for number, tile in enumerate(tiles):
            index, which = places[len(before) + number]
            parts.append(
                softmax_tile(
                    keys_refs[number][:, part],
                    values_ref[value_rows(index, rows), part],
                    qt_ref[which, part, :],
                    bias_ref[index],
                )
            )
        for which, (stat, out) in enumerate(((own_stat, own_acc), (next_stat, next_acc))):
            tops = [
                jnp.where(place[1] == which, one[0], HIDDEN)
                for place, one in zip(places, parts)
            ]
            top = tops[0]
            for one in tops[1:]:
                top = jnp.maximum(top, one)
            total, acc = 0.0, 0.0
            for place, one in zip(places, parts):
                fade = jnp.where(place[1] == which, jnp.exp2(one[0] - top), 0.0)
                total = total + fade * one[1]
                acc = acc + fade * one[2]
            stat[head : head + 1, :] = top
            stat[heads + head : heads + head + 1, :] = total
            stat[2 * heads + head : 2 * heads + head + 1, :] = jnp.sum(
                gt_ref[which, part, :].astype(F32) * acc, axis=0, keepdims=True
            )
            out[part, :] = acc.astype(out.dtype)


def merged(first, second, heads):
    top = jnp.maximum(first[:heads], second[:heads])
    fades = [jnp.exp2(s[:heads] - top) for s in (first, second)]
    total = fades[0] * first[heads : 2 * heads] + fades[1] * second[heads : 2 * heads]
    inverse = 1.0 / total
    fades = [fade * inverse for fade in fades]
    delta = fades[0] * first[2 * heads : 3 * heads] + fades[1] * second[2 * heads : 3 * heads]
    return stacked([top + jnp.log2(total), delta, *fades])


def value_grad_kernel(
    tiles,
    where_ref,
    bias_ref,
    own_stat,
    next_stat,
    before_stat,
    after_stat,
    qt_ref,
    g_both,
    *refs,
):
    keys_refs = refs[: len(tiles)]
    final_ref, dv_ref = refs[len(tiles) :]
    rows = bias_ref.shape[-1]
    heads = dv_ref.shape[1] // HEAD_DIM
    final_ref[0] = merged(own_stat[...], before_stat[...], heads)
    final_ref[1] = merged(next_stat[...], after_stat[...], heads)
    for number, tile in enumerate(tiles):
        index, which = tile_place(where_ref, tile)
        for head in range(heads):
            part = lanes(head)
            raw = dot(keys_refs[number][:, part], qt_ref[which, part, :]) * (SCALE * LOG2E)
            shift = bias_ref[index] - final_ref[which, head : head + 1, :]
            weight = stacked(
                [
                    jnp.exp2(
                        raw[block * BLOCK : (block + 1) * BLOCK] + shift[block : block + 1]
                    ).astype(BF16)
                    for block in range(rows // BLOCK)
                ]
            )
            dv_ref[value_rows(index, rows), part] = dot(weight, g_both[which, :, part]).astype(BF16)


def key_grad_kernel(tiles, first, last, where_ref, bias_ref, final_ref, *refs):
    refs = list(refs)
    count = len(tiles)
    take = lambda number: [refs.pop(0) for _ in range(number)]
    q_both, qt_ref, gt_ref, values_ref = take(4)
    if not first:
        (dq_in,) = take(1)
    if last:
        g_both, noisy_values_ref = take(2)
    keys_refs = take(count)
    dk_refs = take(count)
    if last:
        noisy_dv_ref, own_dq, next_dq, dq_ref = take(4)
    else:
        (dq_ref,) = take(1)
    rows = bias_ref.shape[-1]
    heads = values_ref.shape[1] // HEAD_DIM
    dq_ref[...] = jnp.zeros_like(dq_ref) if first else dq_in[...]
    for number, tile in enumerate(tiles):
        index, which = tile_place(where_ref, tile)
        for head in range(heads):
            part = lanes(head)
            keys = keys_refs[number][:, part]
            if tile is NOISY:
                values = noisy_values_ref[:, part]
            else:
                values = values_ref[value_rows(index, rows), part]
            raw = dot(keys, qt_ref[which, part, :]) * (SCALE * LOG2E)
            dweight = dot(values, gt_ref[which, part, :])
            shift = bias_ref[index] - final_ref[which, head : head + 1, :]
            delta = final_ref[which, heads + head : heads + head + 1, :]
            weights, dscores = [], []
            for block in range(rows // BLOCK):
                here = slice(block * BLOCK, (block + 1) * BLOCK)
                weight = jnp.exp2(raw[here] + shift[block : block + 1])
                weights.append(weight.astype(BF16))
                dscores.append((weight * (dweight[here] - delta)).astype(BF16))
            dscore = stacked(dscores)
            dk = dot(dscore, q_both[which, :, part])
            dk_refs[number][:, part] = dk.astype(dk_refs[number].dtype)
            dq_ref[which, part, :] += dot(keys.T, dscore)
            if tile is NOISY:
                noisy_dv_ref[:, part] = dot(stacked(weights), g_both[0, :, part]).astype(BF16)
    if last:
        for head in range(heads):
            part = lanes(head)
            own_dq[:, part] = dq_ref[0, part, :].T
            next_dq[:, part] = dq_ref[1, part, :].T.astype(BF16)


def finish_kernel(final_ref, acc_ref, acc_before_ref, dq_ref, dq_before_ref, out_ref, dq_out):
    heads = dq_ref.shape[1] // HEAD_DIM
    dq_out[...] = dq_ref[...] + dq_before_ref[...].astype(F32)
    for head in range(heads):
        part = lanes(head)
        row = lambda kind: final_ref[0, kind * heads + head : kind * heads + head + 1, :]
        output = acc_ref[part, :] * row(2) + acc_before_ref[part, :].astype(F32) * row(3)
        out_ref[:, part] = output.T.astype(BF16)


def call(body, name, outs, flops, *operands, unread=(), where=None, scratch=()):
    outs = [jax.ShapeDtypeStruct(shape, dtype) for shape, dtype in outs]
    sizes = [o.size * o.dtype.itemsize for o in (*operands, *outs)]
    scalars = () if where is None else (where,)
    operands = (*unread, *scalars, *operands)
    return pl.pallas_call(
        body,
        name=name,
        in_specs=[pl.BlockSpec(memory_space=pl.ANY)] * len(unread)
        + [pl.BlockSpec(memory_space=pltpu.SMEM)] * len(scalars)
        + [pl.BlockSpec(memory_space=pltpu.VMEM)] * (len(operands) - len(unread) - len(scalars)),
        out_specs=[pl.BlockSpec(memory_space=pltpu.VMEM)] * len(outs),
        out_shape=outs,
        scratch_shapes=scratch,
        compiler_params=pltpu.CompilerParams(vmem_limit_bytes=48 * 1024 * 1024),
        cost_estimate=pl.CostEstimate(
            flops=flops, bytes_accessed=sum(sizes), transcendentals=flops // 512
        ),
    )(*operands)


def row_sum(wide):
    folded = wide[:, lanes(0)]
    for head in range(1, wide.shape[1] // HEAD_DIM):
        folded = folded + wide[:, lanes(head)]
    return jnp.sum(folded.T, axis=0, keepdims=True)


def unit_kernel(full_width, raw_ref, totals_ref, gain_ref, out_ref):
    inverse = lax.rsqrt(totals_ref[...] / full_width + EPS).T
    out_ref[...] = (raw_ref[...].astype(F32) * inverse[:, :1] * gain_ref[...]).astype(BF16)


def inner_kernel(
    query_ref,
    noisy_ref,
    clean_ref,
    query_gain_ref,
    key_gain_ref,
    dq_ref,
    dkn_ref,
    dkc_ref,
    one_ref,
    other_ref,
    total_ref,
    inner_ref,
):
    total = dkc_ref[...] + one_ref[...].astype(F32) + other_ref[...].astype(F32)
    total_ref[...] = total
    inner_ref[...] = jnp.zeros_like(inner_ref)
    for index, (raw_ref, gain_ref, grad) in enumerate(
        (
            (clean_ref, key_gain_ref, total),
            (query_ref, query_gain_ref, dq_ref[...]),
            (noisy_ref, key_gain_ref, dkn_ref[...]),
        )
    ):
        inner_ref[index : index + 1, :] = row_sum(
            raw_ref[...].astype(F32) * (gain_ref[...] * (grad * SCALE))
        )


def unit_backward(values, inverse, term, inner, full_width):
    return (inverse[:, None] * term - values * (inverse**3 * inner / full_width)[:, None]).astype(
        BF16
    )


def local(
    queries,
    noisy_keys,
    noisy_values,
    clean_keys,
    clean_values,
    query_gain,
    key_gain,
    first_block,
    loss_mask,
    grad_output,
):
    row_count, local_width = queries.shape
    full_width = local_width * lax.axis_size("head")
    shard_count = lax.axis_size("seq")
    shard_index = lax.axis_index("seq")
    place = shard_index % RING
    block_count = row_count // BLOCK
    heads = local_width // HEAD_DIM
    wide = (row_count, local_width)
    turned = (local_width, row_count)
    both, both_turned = (2, *wide), (2, *turned)
    tile_flops = 2 * row_count * row_count * local_width

    values = ring_gather(clean_values)
    grad_masked = grad_output * loss_mask[:, None].astype(BF16)
    grad_next = shifted(grad_masked, -RING)
    first_next = shifted(first_block, -RING)

    query_raw = queries.astype(F32)
    noisy_raw = noisy_keys.astype(F32)
    clean_raw = clean_keys.astype(F32)
    totals = head_sum(
        jnp.concatenate(
            [
                jnp.sum(clean_raw * clean_raw, axis=1)[None],
                jnp.sum(query_raw * query_raw, axis=1)[None],
                jnp.sum(noisy_raw * noisy_raw, axis=1)[None],
                jnp.zeros((5, row_count), F32),
            ],
            axis=0,
        )
    )
    key_gain_row, query_gain_row = key_gain[None, :], query_gain[None, :]
    (clean_unit,) = call(
        partial(unit_kernel, float(full_width)),
        "unit",
        [(wide, BF16)],
        1 << 20,
        clean_keys,
        totals,
        key_gain_row,
    )
    first = (swapped(clean_unit, 0), swapped(clean_unit, 1))
    second = (swapped(first[1], 0), swapped(first[0], 1))
    third = (swapped(second[1], 0), swapped(second[0], 1))
    fourth = swapped(third[1], 0)

    inverse = lax.rsqrt(totals[:3] / full_width + EPS)
    clean_inverse, query_inverse, noisy_inverse = inverse[0], inverse[1], inverse[2]
    query_unit = (query_raw * query_inverse[:, None] * query_gain[None, :]).astype(BF16)
    noisy_unit = (noisy_raw * noisy_inverse[:, None] * key_gain[None, :]).astype(BF16)
    query_next = shifted(query_unit, -RING)

    def block_of(shard):
        return (shard * block_count + jnp.arange(row_count, dtype=jnp.int32) // BLOCK)[
            None, None, :
        ]

    def first_of(blocks):
        return jnp.repeat(blocks, BLOCK)[None, None, :]

    query_block = block_of(shard_index)
    next_block = block_of((shard_index + RING) % shard_count)
    places = jnp.arange(RING, dtype=jnp.int32)
    block_row = jnp.arange(block_count, dtype=jnp.int32)
    key_block = ((shard_index - place + places)[:, None] * block_count + block_row[None, :])[
        :, :, None
    ]
    seen = jnp.where(
        (places > place)[:, None, None],
        (key_block < next_block) & (key_block >= first_of(first_next)),
        (key_block < query_block) & (key_block >= first_of(first_block)),
    )
    own_block = (shard_index * block_count + block_row)[None, :, None]
    seen = jnp.concatenate([seen, own_block == query_block], axis=0)
    bias = jnp.where(seen, 0.0, HIDDEN).astype(F32)
    where = jnp.stack([place, place % 2]).astype(jnp.int32)

    early = [NOISY, OWN, *FIRST, *SECOND]
    late = [*THIRD, FOURTH]
    query_t, grad_t, q_both, g_both, stat, acc = call(
        partial(forward_kernel, early),
        "forward",
        [
            (both_turned, BF16),
            (both_turned, BF16),
            (both, BF16),
            (both, BF16),
            ((2 * len(early), heads, row_count), F32),
            ((len(early), *turned), F32),
        ],
        2 * len(early) * tile_flops,
        bias,
        query_unit,
        query_next,
        grad_masked,
        grad_next,
        noisy_values,
        values,
        noisy_unit,
        clean_unit,
        *first,
        *second,
        where=where,
    )
    stat_rows = (3 * heads, row_count)
    own_stat, next_stat, own_acc, next_acc = call(
        partial(forward_end_kernel, late, early),
        "forward",
        [(stat_rows, F32), (stat_rows, F32), (turned, F32), (turned, BF16)],
        4 * len(late) * tile_flops,
        bias,
        query_t,
        grad_t,
        stat,
        acc,
        values,
        *third,
        fourth,
        where=where,
    )
    before_stat = shifted(next_stat, RING)
    after_stat = shifted(own_stat, -RING)
    final, value_parts = call(
        partial(value_grad_kernel, [FOURTH, *THIRD, *SECOND, *FIRST, OWN]),
        "value_grad",
        [((2, 4 * heads, row_count), F32), ((RING * row_count, local_width), BF16)],
        2 * RING * tile_flops,
        bias,
        own_stat,
        next_stat,
        before_stat,
        after_stat,
        query_t,
        g_both,
        fourth,
        *third,
        *second,
        *first,
        clean_unit,
        where=where,
    )
    grad_clean_values = ring_scatter(value_parts)

    def key_grads(tiles, keys, types, carried):
        return call(
            partial(key_grad_kernel, tiles, not carried, False),
            "key_grad",
            [*[(wide, t) for t in types], (both_turned, F32)],
            4 * len(tiles) * tile_flops,
            bias,
            final,
            q_both,
            query_t,
            grad_t,
            values,
            *carried,
            *keys,
            where=where,
        )

    def joined(arrived, part):
        return (arrived.astype(F32) + part).astype(BF16)

    grad_fourth, grad_a3, grad_b3, *carried = key_grads(
        [FOURTH, *THIRD], (fourth, *third), [BF16, BF16, F32], ()
    )
    back_fourth = swapped(grad_fourth, 0)
    back_a3 = swapped(grad_a3, 0)
    grad_a2, grad_b2, *carried = key_grads(SECOND, second, [F32, F32], carried)
    back_b3 = swapped(joined(back_fourth, grad_b3), 1)
    grad_a1, grad_b1, *carried = key_grads(FIRST, first, [F32, F32], carried)
    back_b2 = swapped(joined(back_a3, grad_b2), 1)
    back_a2 = swapped(joined(back_b3, grad_a2), 0)
    back_a1 = swapped(joined(back_b2, grad_a1), 0)
    back_b1 = swapped(joined(back_a2, grad_b1), 1)
    own_key, noisy_key, noisy_value, own_dq, next_dq = call(
        partial(key_grad_kernel, [OWN, NOISY], False, True),
        "key_grad",
        [(wide, F32), (wide, F32), (wide, BF16), (wide, F32), (wide, BF16)],
        9 * tile_flops,
        bias,
        final,
        q_both,
        query_t,
        grad_t,
        values,
        *carried,
        g_both,
        noisy_values,
        clean_unit,
        noisy_unit,
        where=where,
        scratch=[pltpu.VMEM(both_turned, F32)],
    )
    acc_before = shifted(next_acc, RING)
    dq_before = shifted(next_dq, RING)
    attended, query_grad = call(
        finish_kernel,
        "finish",
        [(wide, BF16), (wide, F32)],
        1 << 20,
        final,
        own_acc,
        acc_before,
        own_dq,
        dq_before,
    )
    clean_grad, inner = call(
        inner_kernel,
        "inner",
        [(wide, F32), ((8, row_count), F32)],
        1 << 20,
        queries,
        noisy_keys,
        clean_keys,
        query_gain_row,
        key_gain_row,
        query_grad,
        noisy_key,
        own_key,
        back_a1,
        back_b1,
    )
    inner = head_sum(inner, (grad_clean_values,))

    query_term = query_gain[None, :] * (query_grad * SCALE)
    noisy_term = key_gain[None, :] * (noisy_key * SCALE)
    clean_term = key_gain[None, :] * (clean_grad * SCALE)
    grad_clean_keys = unit_backward(clean_raw, clean_inverse, clean_term, inner[0], full_width)
    grad_queries = unit_backward(query_raw, query_inverse, query_term, inner[1], full_width)
    grad_noisy_keys = unit_backward(noisy_raw, noisy_inverse, noisy_term, inner[2], full_width)
    return (
        attended,
        grad_queries,
        grad_noisy_keys,
        noisy_value,
        grad_clean_keys,
        grad_clean_values,
    )


def solution(mesh):
    spread = P("seq", "head")
    in_specs = (
        spread,
        spread,
        spread,
        spread,
        spread,
        P("head"),
        P("head"),
        P("seq"),
        P("seq"),
        spread,
    )
    return jax.shard_map(
        local, mesh=mesh, in_specs=in_specs, out_specs=(spread,) * 6, check_vma=False
    )
```

time: 284 us -> 208 us (0.73)
  the two profiles are of different devices: /device:TPU:142 before, /device:TPU:6 now
where the time goes in v1:
time: 208 us; the launch traced here: 207 us
  starting transfers between devices  85 us (41%)
  waiting for transfers between devices  48.7 us (23%)
  Pallas kernels  38.3 us (18%)
  between operations  14.9 us (7%)
  local copies, waits for them, and re-layouts  11.5 us (6%)
  other arithmetic  8.84 us (4%)
    ppermute x14, starting transfers between devices, swapped(): return lax.ppermute(shard, 'seq', pairs)  47.8 us
    pallas_call x11, Pallas kernels, call(): pl.pallas_call(body, name=name, in_specs=[pl.BlockSpec(memory_space=pl.AN...  38.3 us
    ppermute x14, waiting for transfers between devices, swapped(): return lax.ppermute(shard, 'seq', pairs)  29.2 us
    ppermute x7, starting transfers between devices, shifted(): lax.ppermute(shard, 'seq', [(i, (i + by) % count) for i in range(count)])  21.7 us
    ppermute x6, starting transfers between devices, head_sum(): other = lax.ppermute(values, 'head', [(i, i ^ bit) for i in range(count)])  15.3 us
    ppermute x6, waiting for transfers between devices, head_sum(): other = lax.ppermute(values, 'head', [(i, i ^ bit) for i in range(count)])  14.6 us
    unnamed x78, local copies, waits for them, and re-layouts  11.1 us
    ppermute x7, waiting for transfers between devices, shifted(): lax.ppermute(shard, 'seq', [(i, (i + by) % count) for i in range(count)])  4.18 us
  transfers between devices with their start and end apart: 29, of which 15 were waited for; matrix products, arithmetic and copies ran while one was open for 4% of the time, Pallas kernels for 14%

profile of v1, /device:TPU:6, one launch (start us, length us, event | category | flops | bytes accessed | tf_op | source)
XLA Modules:
  0.0 207.1 jit_solution(10893106362308280672)
XLA Ops:
  8.0 5.4 %collective-permute-start = (s32[8]{0:T(128)}, s32[8]{0:T(128)S(1)}, u32[]{:S(2)}, u32[]{:S(2)}) collective-permute-start(s32[8]{0:T(128)} %param.17), channel_id=1, source_target_pairs={{0,448},{8,456},{16,464},{24,472},{32,480},{40,488},{48,496},{56,5... | collective-permute-start | bytes 104 | tf_op jit(solution)/shard_map/ppermute | solution.py:29
  20.5 3.3 %collective-permute-start.5 = (bf16[256,512]{1,0:T(8,128)(2,1)S(1)}, bf16[256,512]{1,0:T(8,128)(2,1)}, u32[]{:S(2)}, u32[]{:S(2)}) collective-permute-start(bf16[256,512]{1,0:T(8,128)(2,1)S(1)} %broadcast_multiply_fusion.g_ref), channel_id=1, source_target_pairs={{0,448},{8,456},{16,464},{24,472},{32,480},{40,488},{48,496},{56,5... | collective-permute-start | bytes 786440 | tf_op jit(solution)/shard_map/ppermute | solution.py:29
  23.9 2.7 %collective-permute-start.2 = (f32[8,256]{1,0:T(8,128)S(1)}, f32[8,256]{1,0:T(8,128)S(1)}, u32[]{:S(2)}, u32[]{:S(2)}) collective-permute-start(f32[8,256]{1,0:T(8,128)S(1)} %fusion.22), channel_id=1, source_target_pairs={{0,2},{1,3},{2,0},{3,1},{4,6},{5,7},{6,4},{7,5},{8,10},{9,11},{10,... | collective-permute-start | bytes 24584 | tf_op jit(solution)/shard_map/ppermute | solution.py:67
  26.8 2.7 %collective-permute-done.2 = f32[8,256]{1,0:T(8,128)S(1)} collective-permute-done((f32[8,256]{1,0:T(8,128)S(1)}, f32[8,256]{1,0:T(8,128)S(1)}, u32[]{:S(2)}, u32[]{:S(2)}) %collective-permute-start.2) | collective-permute-done | bytes 8224 | tf_op jit(solution)/shard_map/ppermute | solution.py:67
  29.6 3.3 %collective-permute-start.3 = (f32[8,256]{1,0:T(8,128)S(1)}, f32[8,256]{1,0:T(8,128)S(1)}, u32[]{:S(2)}, u32[]{:S(2)}) collective-permute-start(f32[8,256]{1,0:T(8,128)S(1)} %fusion.25), channel_id=1, source_target_pairs={{0,4},{1,5},{2,6},{3,7},{4,0},{5,1},{6,2},{7,3},{8,12},{9,13},{10,... | collective-permute-start | bytes 24584 | tf_op jit(solution)/shard_map/ppermute | solution.py:67
  32.9 3.7 %collective-permute-done.3 = f32[8,256]{1,0:T(8,128)S(1)} collective-permute-done((f32[8,256]{1,0:T(8,128)S(1)}, f32[8,256]{1,0:T(8,128)S(1)}, u32[]{:S(2)}, u32[]{:S(2)}) %collective-permute-start.3) | collective-permute-done | bytes 8224 | tf_op jit(solution)/shard_map/ppermute | solution.py:67
  38.5 10.9 %collective-permute-start.7 = (bf16[256,512]{1,0:T(8,128)(2,1)S(1)}, bf16[256,512]{1,0:T(8,128)(2,1)S(1)}, u32[]{:S(2)}, u32[]{:S(2)}) collective-permute-start(bf16[256,512]{1,0:T(8,128)(2,1)S(1)} %unit.1.refs_1_.refs_7_), channel_id=1, source_target_pairs={{8,16},{16,8},{24,32},{32,24},{40,48},{48,40},{56,0},{0,56},{72,80... | collective-permute-start | bytes 786440 | tf_op jit(solution)/shard_map/ppermute | solution.py:53
  51.9 8.6 %collective-permute-done.7.refs_3_.refs_6_ = bf16[256,512]{1,0:T(8,128)(2,1)S(1)} collective-permute-done((bf16[256,512]{1,0:T(8,128)(2,1)S(1)}, bf16[256,512]{1,0:T(8,128)(2,1)S(1)}, u32[]{:S(2)}, u32[]{:S(2)}) %collective-permute-start.7) | collective-permute-done | bytes 262176 | tf_op jit(solution)/shard_map/ppermute | solution.py:53
  63.1 3.5 %collective-permute-start.9 = (bf16[256,512]{1,0:T(8,128)(2,1)S(1)}, bf16[256,512]{1,0:T(8,128)(2,1)S(1)}, u32[]{:S(2)}, u32[]{:S(2)}) collective-permute-start(bf16[256,512]{1,0:T(8,128)(2,1)S(1)} %collective-permute-done.6.refs_2_.refs_5_), channel_id=1, source_target_pairs={{8,16},{16,8},{24,32},{32,24},{40,48},{48,40},{56,0},{0,56},{72,80... | collective-permute-start | bytes 786440 | tf_op jit(solution)/shard_map/ppermute | solution.py:53
  69.4 3.8 %collective-permute-start.11 = (bf16[256,512]{1,0:T(8,128)(2,1)S(1)}, bf16[256,512]{1,0:T(8,128)(2,1)S(1)}, u32[]{:S(2)}, u32[]{:S(2)}) collective-permute-start(bf16[256,512]{1,0:T(8,128)(2,1)S(1)} %collective-permute-done.8.refs_4_.refs_3_.refs_5_), channel_id=1, source_target_pairs={{8,16},{16,8},{24,32},{32,24},{40,48},{48,40},{56,0},{0,56},{72,80... | collective-permute-start | bytes 786440 | tf_op jit(solution)/shard_map/ppermute | solution.py:53
  73.4 3.1 %collective-permute-start.4 = (bf16[256,512]{1,0:T(8,128)(2,1)S(1)}, bf16[256,512]{1,0:T(8,128)(2,1)S(1)}, u32[]{:S(2)}, u32[]{:S(2)}) collective-permute-start(bf16[256,512]{1,0:T(8,128)(2,1)S(1)} %fusion.5.q_ref), channel_id=1, source_target_pairs={{0,448},{8,456},{16,464},{24,472},{32,480},{40,488},{48,496},{56,5... | collective-permute-start | bytes 786440 | tf_op jit(solution)/shard_map/ppermute | solution.py:29
  78.8 3.6 %collective-permute-start.12 = (bf16[256,512]{1,0:T(8,128)(2,1)S(1)}, bf16[256,512]{1,0:T(8,128)(2,1)S(1)}, u32[]{:S(2)}, u32[]{:S(2)}) collective-permute-start(bf16[256,512]{1,0:T(8,128)(2,1)S(1)} %collective-permute-done.11.refs_1_.refs_2_.refs_6_), channel_id=1, source_target_pairs={{0,8},{8,0},{16,24},{24,16},{32,40},{40,32},{48,56},{56,48},{64,72... | collective-permute-start | bytes 786440 | tf_op jit(solution)/shard_map/ppermute | solution.py:53
  88.8 10.5 %forward.2 = (bf16[2,512,256]{2,1,0:T(8,128)(2,1)S(1)}, bf16[2,512,256]{2,1,0:T(8,128)(2,1)S(1)}, bf16[2,256,512]{2,1,0:T(8,128)(2,1)S(1)}, bf16[2,256,512]{2,1,...) custom-call(s32[2]{0:T(128)S(1)} %pad_add_fusion.where_ref, ...), custom_call_target="tpu_custom_call" | custom-call | flops 805306368 | bytes 10346496 | tf_op jit(solution)/shard_map/forward/pallas_call | solution.py:327
  100.1 6.9 %forward.3 = (f32[12,256]{1,0:T(8,128)S(1)}, f32[12,256]{1,0:T(8,128)S(1)}, f32[512,256]{1,0:T(8,128)S(1)}, bf16[512,256]{1,0:T(8,128)(2,1)S(1)}) custom-call(s32[2]{0:T(128)S(1)} %pad_add_fusion.where_ref, f32[9,8,256]{2,1,0:T(8,128)S(1)} %add_select_fusion.bias_ref, bf16[2,512,256]{2,1,0:T(8,128)(2,1)S(1)} %get-tuple-element.37.qt_ref.refs_1_, ...), custom_call_target="tpu_custom_call" | custom-call | flops 805306368 | bytes 8011776 | tf_op jit(solution)/shard_map/forward/pallas_call | solution.py:327
  107.8 3.0 %collective-permute-start.14 = (f32[12,256]{1,0:T(8,128)S(1)}, f32[12,256]{1,0:T(8,128)S(1)}, u32[]{:S(2)}, u32[]{:S(2)}) collective-permute-start(f32[12,256]{1,0:T(8,128)S(1)} %get-tuple-element.41.own_stat), channel_id=1, source_target_pairs={{0,448},{8,456},{16,464},{24,472},{32,480},{40,488},{48,496},{56,5... | collective-permute-start | bytes 36872 | tf_op jit(solution)/shard_map/ppermute | solution.py:29
  110.8 3.0 %collective-permute-start.13 = (f32[12,256]{1,0:T(8,128)S(1)}, f32[12,256]{1,0:T(8,128)S(1)}, u32[]{:S(2)}, u32[]{:S(2)}) collective-permute-start(f32[12,256]{1,0:T(8,128)S(1)} %get-tuple-element.42.next_stat), channel_id=1, source_target_pairs={{0,64},{8,72},{16,80},{24,88},{32,96},{40,104},{48,112},{56,120},{... | collective-permute-start | bytes 36872 | tf_op jit(solution)/shard_map/ppermute | solution.py:29
  113.9 3.8 %collective-permute-done.13.before_stat = f32[12,256]{1,0:T(8,128)S(1)} collective-permute-done((f32[12,256]{1,0:T(8,128)S(1)}, f32[12,256]{1,0:T(8,128)S(1)}, u32[]{:S(2)}, u32[]{:S(2)}) %collective-permute-start.13) | collective-permute-done | bytes 12320 | tf_op jit(solution)/shard_map/ppermute | solution.py:29
  117.7 3.0 %value_grad.1 = (f32[2,16,256]{2,1,0:T(8,128)S(1)}, bf16[2048,512]{1,0:T(8,128)(2,1)S(1)}) custom-call(s32[2]{0:T(128)S(1)} %pad_add_fusion.where_ref, f32[9,8,256]{2,1,0:T(8,128)S(1)} %add_select_fusion.bias_ref, f32[12,256]{1,0:T(8,128)S(1)} %get-tuple-element.41.own_stat, f32[12,256]{1,0:T(8,128)S(1)} %get-tuple-element.42.next_stat, ...), custom_call_target="tpu_custom_call" | custom-call | flops 1073741824 | bytes 5398528 | tf_op jit(solution)/shard_map/value_grad/pallas_call | solution.py:327
  122.1 4.6 %key_grad.4 = (bf16[256,512]{1,0:T(8,128)(2,1)S(1)}, bf16[256,512]{1,0:T(8,128)(2,1)S(1)}, f32[256,512]{1,0:T(8,128)S(1)}, f32[2,512,256]{2,1,0:T(8,128)S(1)}) custom-call(s32[2]{0:T(128)S(1)} %pad_add_fusion.where_ref, f32[9,8,256]{2,1,0:T(8,128)S(1)} %add_select_fusion.bias_ref, f32[2,16,256]{2,1,0:T(8,128)S(1)} %get-tuple-element.44.final_ref, ...), custom_call_target="tpu_custom_call" | custom-call | flops 805306368 | bytes 6660096 | tf_op jit(solution)/shard_map/key_grad/pallas_call | solution.py:327
  126.7 3.7 %collective-permute-start.20 = (bf16[256,512]{1,0:T(8,128)(2,1)S(1)}, bf16[256,512]{1,0:T(8,128)(2,1)S(1)}, u32[]{:S(2)}, u32[]{:S(2)}) collective-permute-start(bf16[256,512]{1,0:T(8,128)(2,1)S(1)} %get-tuple-element.61), channel_id=1, source_target_pairs={{0,8},{8,0},{16,24},{24,16},{32,40},{40,32},{48,56},{56,48},{64,72... | collective-permute-start | bytes 786440 | tf_op jit(solution)/shard_map/ppermute | solution.py:53
  134.5 3.6 %key_grad.5 = (f32[256,512]{1,0:T(8,128)S(1)}, f32[256,512]{1,0:T(8,128)S(1)}, f32[2,512,256]{2,1,0:T(8,128)S(1)}) custom-call(s32[2]{0:T(128)S(1)} %pad_add_fusion.where_ref, f32[9,8,256]{2,1,0:T(8,128)S(1)} %add_select_fusion.bias_ref, f32[2,16,256]{2,1,0:T(8,128)S(1)} %get-tuple-element.44.final_ref, bf16[2,256,512]{2,1,0:T(8,128)(2,1)S(1)} %copy-done.2, ...), custom_call_target="tpu_custom_call" | custom-call | flops 536870912 | bytes 7446528 | tf_op jit(solution)/shard_map/key_grad/pallas_call | solution.py:327
  138.1 3.6 %collective-permute-done.20 = bf16[256,512]{1,0:T(8,128)(2,1)S(1)} collective-permute-done((bf16[256,512]{1,0:T(8,128)(2,1)S(1)}, bf16[256,512]{1,0:T(8,128)(2,1)S(1)}, u32[]{:S(2)}, u32[]{:S(2)}) %collective-permute-start.20) | collective-permute-done | bytes 262176 | tf_op jit(solution)/shard_map/ppermute | solution.py:53
  144.5 3.6 %key_grad.6 = (f32[256,512]{1,0:T(8,128)S(1)}, f32[256,512]{1,0:T(8,128)S(1)}, f32[2,512,256]{2,1,0:T(8,128)S(1)}) custom-call(s32[2]{0:T(128)S(1)} %pad_add_fusion.where_ref, f32[9,8,256]{2,1,0:T(8,128)S(1)} %add_select_fusion.bias_ref, f32[2,16,256]{2,1,0:T(8,128)S(1)} %get-tuple-element.44.final_ref, bf16[2,256,512]{2,1,0:T(8,128)(2,1)S(1)} %copy-done.2, ...), custom_call_target="tpu_custom_call" | custom-call | flops 536870912 | bytes 7446528 | tf_op jit(solution)/shard_map/key_grad/pallas_call | solution.py:327
  150.2 2.7 %collective-permute-start.18 = (bf16[256,512]{1,0:T(8,128)(2,1)S(1)}, bf16[256,512]{1,0:T(8,128)(2,1)S(1)}, u32[]{:S(2)}, u32[]{:S(2)}) collective-permute-start(bf16[256,512]{1,0:T(8,128)(2,1)S(1)} %add_convert_fusion.4), channel_id=1, source_target_pairs={{8,16},{16,8},{24,32},{32,24},{40,48},{48,40},{56,0},{0,56},{72,80... | collective-permute-start | bytes 786440 | tf_op jit(solution)/shard_map/ppermute | solution.py:53
  152.9 6.1 %collective-permute-done.21 = bf16[256,512]{1,0:T(8,128)(2,1)S(1)} collective-permute-done((bf16[256,512]{1,0:T(8,128)(2,1)S(1)}, bf16[256,512]{1,0:T(8,128)(2,1)S(1)}, u32[]{:S(2)}, u32[]{:S(2)}) %collective-permute-start.21) | collective-permute-done | bytes 262176 | tf_op jit(solution)/shard_map/ppermute | solution.py:53
  161.0 4.6 %key_grad.7 = (f32[256,512]{1,0:T(8,128)S(1)}, f32[256,512]{1,0:T(8,128)S(1)}, bf16[256,512]{1,0:T(8,128)(2,1)}, f32[256,512]{1,0:T(8,128)S(1)}, bf16[256,512]{1,0:T(8,128)(2,1)S(1)}) custom-call(s32[2]{0:T(128)S(1)} %pad_add_fusion.where_ref, f32[9,8,256]{2,1,0:T(8,128)S(1)} %add_select_fusion.bias_ref, f32[2,16,256]{2,1,0:T(8,128)S(1)} %get-tuple-element.44.final_ref, ...), custom_call_target="tpu_custom_call" | custom-call | flops 603979776 | bytes 8232960 | tf_op jit(solution)/shard_map/key_grad/pallas_call | solution.py:327
  167.8 3.9 %collective-permute-start.19 = (bf16[256,512]{1,0:T(8,128)(2,1)S(1)}, bf16[256,512]{1,0:T(8,128)(2,1)S(1)}, u32[]{:S(2)}, u32[]{:S(2)}) collective-permute-start(bf16[256,512]{1,0:T(8,128)(2,1)S(1)} %add_convert_fusion.3), channel_id=1, source_target_pairs={{0,8},{8,0},{16,24},{24,16},{32,40},{40,32},{48,56},{56,48},{64,72... | collective-permute-start | bytes 786440 | tf_op jit(solution)/shard_map/ppermute | solution.py:53
  171.8 3.1 %collective-permute-start.23 = (bf16[256,512]{1,0:T(8,128)(2,1)S(1)}, bf16[256,512]{1,0:T(8,128)(2,1)S(1)}, u32[]{:S(2)}, u32[]{:S(2)}) collective-permute-start(bf16[256,512]{1,0:T(8,128)(2,1)S(1)} %add_convert_fusion), channel_id=1, source_target_pairs={{8,16},{16,8},{24,32},{32,24},{40,48},{48,40},{56,0},{0,56},{72,80... | collective-permute-start | bytes 786440 | tf_op jit(solution)/shard_map/ppermute | solution.py:53
  176.1 5.2 %collective-permute-done.23.other_ref = bf16[256,512]{1,0:T(8,128)(2,1)S(1)} collective-permute-done((bf16[256,512]{1,0:T(8,128)(2,1)S(1)}, bf16[256,512]{1,0:T(8,128)(2,1)S(1)}, u32[]{:S(2)}, u32[]{:S(2)}) %collective-permute-start.23) | collective-permute-done | bytes 262176 | tf_op jit(solution)/shard_map/ppermute | solution.py:53
  187.1 3.2 %collective-permute-done.25.refs_2_ = f32[8,256]{1,0:T(8,128)S(1)} collective-permute-done((f32[8,256]{1,0:T(8,128)S(1)}, f32[8,256]{1,0:T(8,128)S(1)}, u32[]{:S(2)}, u32[]{:S(2)}) %collective-permute-start.25) | collective-permute-done | bytes 8224 | tf_op jit(solution)/shard_map/ppermute | solution.py:67
  191.2 3.2 %collective-permute-start.26 = (f32[8,256]{1,0:T(8,128)S(1)}, f32[8,256]{1,0:T(8,128)S(1)}, u32[]{:S(2)}, u32[]{:S(2)}) collective-permute-start(f32[8,256]{1,0:T(8,128)S(1)} %add.170), channel_id=1, source_target_pairs={{0,4},{1,5},{2,6},{3,7},{4,0},{5,1},{6,2},{7,3},{8,12},{9,13},{10,... | collective-permute-start | bytes 24584 | tf_op jit(solution)/shard_map/ppermute | solution.py:67
  194.4 3.9 %collective-permute-done.26 = f32[8,256]{1,0:T(8,128)S(1)} collective-permute-done((f32[8,256]{1,0:T(8,128)S(1)}, f32[8,256]{1,0:T(8,128)S(1)}, u32[]{:S(2)}, u32[]{:S(2)}) %collective-permute-start.26) | collective-permute-done | bytes 8224 | tf_op jit(solution)/shard_map/ppermute | solution.py:67
  (160 shorter events, 52.5 us)
Async XLA Ops:
  7.2 75.2 %copy-start.3 = (bf16[256,512]{1,0:T(8,128)(2,1)S(1)}, bf16[256,512]{1,0:T(8,128)(2,1)}, u32[]{:S(2)}) copy-start(bf16[256,512]{1,0:T(8,128)(2,1)} %noisy_ref.1) | copy-start | bytes 786436
  7.2 75.2 %copy-start.34 = (f32[512]{0:T(512)S(1)}, f32[512]{0:T(512)}, u32[]{:S(2)}) copy-start(f32[512]{0:T(512)} %param.16) | copy-start | bytes 6148
  7.2 76.8 %copy-start.15 = (bf16[256,512]{1,0:T(8,128)(2,1)S(1)}, bf16[256,512]{1,0:T(8,128)(2,1)}, u32[]{:S(2)}) copy-start(bf16[256,512]{1,0:T(8,128)(2,1)} %refs_6_.1) | copy-start | bytes 786436
  7.2 76.8 %all-gather.2.cloned.1.call-start = ((), (), s32[]{:S(2)}) async-start(), calls=%async_computation.1 | async-start | bytes 2359296 | tf_op jit(solution)/shard_map/all_gather | solution.py:38
  8.0 182.3 %reduce-scatter.2.cloned.1.call-start = ((), (), s32[]{:S(2)}) async-start(), calls=%async_computation.2 | async-start | bytes 2359296 | tf_op jit(solution)/shard_map/reduce_scatter | solution.py:42
  8.0 41.7 %collective-permute-start = (s32[8]{0:T(128)}, s32[8]{0:T(128)S(1)}, u32[]{:S(2)}, u32[]{:S(2)}) collective-permute-start(s32[8]{0:T(128)} %param.17), channel_id=1, source_target_pairs={{0,448},{8,456},{16,464},{24,472},{32,480},{40,488},{48,496},{56,5... | collective-permute-start | bytes 104 | tf_op jit(solution)/shard_map/ppermute | solution.py:29
  16.8 7.1 %collective-permute-start.1 = (f32[8,256]{1,0:T(8,128)S(1)}, f32[8,256]{1,0:T(8,128)S(1)}, u32[]{:S(2)}, u32[]{:S(2)}) collective-permute-start(f32[8,256]{1,0:T(8,128)S(1)} %maximum_maximum_fusion), channel_id=1, source_target_pairs={{0,1},{1,0},{2,3},{3,2},{4,5},{5,4},{6,7},{7,6},{8,9},{9,8},{10,11... | collective-permute-start | bytes 24584 | tf_op jit(solution)/shard_map/ppermute | solution.py:67
  20.5 62.8 %collective-permute-start.5 = (bf16[256,512]{1,0:T(8,128)(2,1)S(1)}, bf16[256,512]{1,0:T(8,128)(2,1)}, u32[]{:S(2)}, u32[]{:S(2)}) collective-permute-start(bf16[256,512]{1,0:T(8,128)(2,1)S(1)} %broadcast_multiply_fusion.g_ref), channel_id=1, source_target_pairs={{0,448},{8,456},{16,464},{24,472},{32,480},{40,488},{48,496},{56,5... | collective-permute-start | bytes 786440 | tf_op jit(solution)/shard_map/ppermute | solution.py:29
  23.9 5.5 %collective-permute-start.2 = (f32[8,256]{1,0:T(8,128)S(1)}, f32[8,256]{1,0:T(8,128)S(1)}, u32[]{:S(2)}, u32[]{:S(2)}) collective-permute-start(f32[8,256]{1,0:T(8,128)S(1)} %fusion.22), channel_id=1, source_target_pairs={{0,2},{1,3},{2,0},{3,1},{4,6},{5,7},{6,4},{7,5},{8,10},{9,11},{10,... | collective-permute-start | bytes 24584 | tf_op jit(solution)/shard_map/ppermute | solution.py:67
  29.6 7.0 %collective-permute-start.3 = (f32[8,256]{1,0:T(8,128)S(1)}, f32[8,256]{1,0:T(8,128)S(1)}, u32[]{:S(2)}, u32[]{:S(2)}) collective-permute-start(f32[8,256]{1,0:T(8,128)S(1)} %fusion.25), channel_id=1, source_target_pairs={{0,4},{1,5},{2,6},{3,7},{4,0},{5,1},{6,2},{7,3},{8,12},{9,13},{10,... | collective-permute-start | bytes 24584 | tf_op jit(solution)/shard_map/ppermute | solution.py:67
  38.5 22.0 %collective-permute-start.7 = (bf16[256,512]{1,0:T(8,128)(2,1)S(1)}, bf16[256,512]{1,0:T(8,128)(2,1)S(1)}, u32[]{:S(2)}, u32[]{:S(2)}) collective-permute-start(bf16[256,512]{1,0:T(8,128)(2,1)S(1)} %unit.1.refs_1_.refs_7_), channel_id=1, source_target_pairs={{8,16},{16,8},{24,32},{32,24},{40,48},{48,40},{56,0},{0,56},{72,80... | collective-permute-start | bytes 786440 | tf_op jit(solution)/shard_map/ppermute | solution.py:53
  50.0 13.2 %collective-permute-start.6 = (bf16[256,512]{1,0:T(8,128)(2,1)S(1)}, bf16[256,512]{1,0:T(8,128)(2,1)S(1)}, u32[]{:S(2)}, u32[]{:S(2)}) collective-permute-start(bf16[256,512]{1,0:T(8,128)(2,1)S(1)} %unit.1.refs_1_.refs_7_), channel_id=1, source_target_pairs={{0,8},{8,0},{16,24},{24,16},{32,40},{40,32},{48,56},{56,48},{64,72... | collective-permute-start | bytes 786440 | tf_op jit(solution)/shard_map/ppermute | solution.py:53
  60.5 8.9 %collective-permute-start.8 = (bf16[256,512]{1,0:T(8,128)(2,1)S(1)}, bf16[256,512]{1,0:T(8,128)(2,1)S(1)}, u32[]{:S(2)}, u32[]{:S(2)}) collective-permute-start(bf16[256,512]{1,0:T(8,128)(2,1)S(1)} %collective-permute-done.7.refs_3_.refs_6_), channel_id=1, source_target_pairs={{0,8},{8,0},{16,24},{24,16},{32,40},{40,32},{48,56},{56,48},{64,72... | collective-permute-start | bytes 786440 | tf_op jit(solution)/shard_map/ppermute | solution.py:53
  63.1 13.4 %collective-permute-start.9 = (bf16[256,512]{1,0:T(8,128)(2,1)S(1)}, bf16[256,512]{1,0:T(8,128)(2,1)S(1)}, u32[]{:S(2)}, u32[]{:S(2)}) collective-permute-start(bf16[256,512]{1,0:T(8,128)(2,1)S(1)} %collective-permute-done.6.refs_2_.refs_5_), channel_id=1, source_target_pairs={{8,16},{16,8},{24,32},{32,24},{40,48},{48,40},{56,0},{0,56},{72,80... | collective-permute-start | bytes 786440 | tf_op jit(solution)/shard_map/ppermute | solution.py:53
  69.4 9.5 %collective-permute-start.11 = (bf16[256,512]{1,0:T(8,128)(2,1)S(1)}, bf16[256,512]{1,0:T(8,128)(2,1)S(1)}, u32[]{:S(2)}, u32[]{:S(2)}) collective-permute-start(bf16[256,512]{1,0:T(8,128)(2,1)S(1)} %collective-permute-done.8.refs_4_.refs_3_.refs_5_), channel_id=1, source_target_pairs={{8,16},{16,8},{24,32},{32,24},{40,48},{48,40},{56,0},{0,56},{72,80... | collective-permute-start | bytes 786440 | tf_op jit(solution)/shard_map/ppermute | solution.py:53
  73.4 9.9 %collective-permute-start.4 = (bf16[256,512]{1,0:T(8,128)(2,1)S(1)}, bf16[256,512]{1,0:T(8,128)(2,1)S(1)}, u32[]{:S(2)}, u32[]{:S(2)}) collective-permute-start(bf16[256,512]{1,0:T(8,128)(2,1)S(1)} %fusion.5.q_ref), channel_id=1, source_target_pairs={{0,448},{8,456},{16,464},{24,472},{32,480},{40,488},{48,496},{56,5... | collective-permute-start | bytes 786440 | tf_op jit(solution)/shard_map/ppermute | solution.py:29
  76.5 23.5 %collective-permute-start.10 = (bf16[256,512]{1,0:T(8,128)(2,1)S(1)}, bf16[256,512]{1,0:T(8,128)(2,1)S(1)}, u32[]{:S(2)}, u32[]{:S(2)}) collective-permute-start(bf16[256,512]{1,0:T(8,128)(2,1)S(1)} %collective-permute-done.9.refs_5_.refs_4_.refs_6_), channel_id=1, source_target_pairs={{0,8},{8,0},{16,24},{24,16},{32,40},{40,32},{48,56},{56,48},{64,72... | collective-permute-start | bytes 786440 | tf_op jit(solution)/shard_map/ppermute | solution.py:53
  78.8 21.2 %collective-permute-start.12 = (bf16[256,512]{1,0:T(8,128)(2,1)S(1)}, bf16[256,512]{1,0:T(8,128)(2,1)S(1)}, u32[]{:S(2)}, u32[]{:S(2)}) collective-permute-start(bf16[256,512]{1,0:T(8,128)(2,1)S(1)} %collective-permute-done.11.refs_1_.refs_2_.refs_6_), channel_id=1, source_target_pairs={{0,8},{8,0},{16,24},{24,16},{32,40},{40,32},{48,56},{56,48},{64,72... | collective-permute-start | bytes 786440 | tf_op jit(solution)/shard_map/ppermute | solution.py:53
  107.8 6.0 %collective-permute-start.14 = (f32[12,256]{1,0:T(8,128)S(1)}, f32[12,256]{1,0:T(8,128)S(1)}, u32[]{:S(2)}, u32[]{:S(2)}) collective-permute-start(f32[12,256]{1,0:T(8,128)S(1)} %get-tuple-element.41.own_stat), channel_id=1, source_target_pairs={{0,448},{8,456},{16,464},{24,472},{32,480},{40,488},{48,496},{56,5... | collective-permute-start | bytes 36872 | tf_op jit(solution)/shard_map/ppermute | solution.py:29
  110.8 6.8 %collective-permute-start.13 = (f32[12,256]{1,0:T(8,128)S(1)}, f32[12,256]{1,0:T(8,128)S(1)}, u32[]{:S(2)}, u32[]{:S(2)}) collective-permute-start(f32[12,256]{1,0:T(8,128)S(1)} %get-tuple-element.42.next_stat), channel_id=1, source_target_pairs={{0,64},{8,72},{16,80},{24,88},{32,96},{40,104},{48,112},{56,120},{... | collective-permute-start | bytes 36872 | tf_op jit(solution)/shard_map/ppermute | solution.py:29
  126.7 15.0 %collective-permute-start.20 = (bf16[256,512]{1,0:T(8,128)(2,1)S(1)}, bf16[256,512]{1,0:T(8,128)(2,1)S(1)}, u32[]{:S(2)}, u32[]{:S(2)}) collective-permute-start(bf16[256,512]{1,0:T(8,128)(2,1)S(1)} %get-tuple-element.61), channel_id=1, source_target_pairs={{0,8},{8,0},{16,24},{24,16},{32,40},{40,32},{48,56},{56,48},{64,72... | collective-permute-start | bytes 786440 | tf_op jit(solution)/shard_map/ppermute | solution.py:53
  130.4 44.5 %collective-permute-start.15 = (bf16[512,256]{1,0:T(8,128)(2,1)S(1)}, bf16[512,256]{1,0:T(8,128)(2,1)S(1)}, u32[]{:S(2)}, u32[]{:S(2)}) collective-permute-start(bf16[512,256]{1,0:T(8,128)(2,1)S(1)} %copy-done.37), channel_id=1, source_target_pairs={{0,64},{8,72},{16,80},{24,88},{32,96},{40,104},{48,112},{56,120},{... | collective-permute-start | bytes 786440 | tf_op jit(solution)/shard_map/ppermute | solution.py:29
  132.3 17.8 %collective-permute-start.17 = (bf16[256,512]{1,0:T(8,128)(2,1)S(1)}, bf16[256,512]{1,0:T(8,128)(2,1)S(1)}, u32[]{:S(2)}, u32[]{:S(2)}) collective-permute-start(bf16[256,512]{1,0:T(8,128)(2,1)S(1)} %get-tuple-element.58), channel_id=1, source_target_pairs={{0,8},{8,0},{16,24},{24,16},{32,40},{40,32},{48,56},{56,48},{64,72... | collective-permute-start | bytes 786440 | tf_op jit(solution)/shard_map/ppermute | solution.py:53
  141.8 17.2 %collective-permute-start.21 = (bf16[256,512]{1,0:T(8,128)(2,1)S(1)}, bf16[256,512]{1,0:T(8,128)(2,1)S(1)}, u32[]{:S(2)}, u32[]{:S(2)}) collective-permute-start(bf16[256,512]{1,0:T(8,128)(2,1)S(1)} %add_convert_fusion.2), channel_id=1, source_target_pairs={{8,16},{16,8},{24,32},{32,24},{40,48},{48,40},{56,0},{0,56},{72,80... | collective-permute-start | bytes 786440 | tf_op jit(solution)/shard_map/ppermute | solution.py:53
  150.2 17.5 %collective-permute-start.18 = (bf16[256,512]{1,0:T(8,128)(2,1)S(1)}, bf16[256,512]{1,0:T(8,128)(2,1)S(1)}, u32[]{:S(2)}, u32[]{:S(2)}) collective-permute-start(bf16[256,512]{1,0:T(8,128)(2,1)S(1)} %add_convert_fusion.4), channel_id=1, source_target_pairs={{8,16},{16,8},{24,32},{32,24},{40,48},{48,40},{56,0},{0,56},{72,80... | collective-permute-start | bytes 786440 | tf_op jit(solution)/shard_map/ppermute | solution.py:53
  159.1 12.6 %collective-permute-start.22 = (bf16[256,512]{1,0:T(8,128)(2,1)S(1)}, bf16[256,512]{1,0:T(8,128)(2,1)S(1)}, u32[]{:S(2)}, u32[]{:S(2)}) collective-permute-start(bf16[256,512]{1,0:T(8,128)(2,1)S(1)} %add_convert_fusion.1), channel_id=1, source_target_pairs={{0,8},{8,0},{16,24},{24,16},{32,40},{40,32},{48,56},{56,48},{64,72... | collective-permute-start | bytes 786440 | tf_op jit(solution)/shard_map/ppermute | solution.py:53
  165.6 9.6 %collective-permute-start.16 = (bf16[256,512]{1,0:T(8,128)(2,1)S(1)}, bf16[256,512]{1,0:T(8,128)(2,1)S(1)}, u32[]{:S(2)}, u32[]{:S(2)}) collective-permute-start(bf16[256,512]{1,0:T(8,128)(2,1)S(1)} %get-tuple-element.52), channel_id=1, source_target_pairs={{0,64},{8,72},{16,80},{24,88},{32,96},{40,104},{48,112},{56,120},{... | collective-permute-start | bytes 786440 | tf_op jit(solution)/shard_map/ppermute | solution.py:29
  167.8 8.3 %collective-permute-start.19 = (bf16[256,512]{1,0:T(8,128)(2,1)S(1)}, bf16[256,512]{1,0:T(8,128)(2,1)S(1)}, u32[]{:S(2)}, u32[]{:S(2)}) collective-permute-start(bf16[256,512]{1,0:T(8,128)(2,1)S(1)} %add_convert_fusion.3), channel_id=1, source_target_pairs={{0,8},{8,0},{16,24},{24,16},{32,40},{40,32},{48,56},{56,48},{64,72... | collective-permute-start | bytes 786440 | tf_op jit(solution)/shard_map/ppermute | solution.py:53
  171.8 9.5 %collective-permute-start.23 = (bf16[256,512]{1,0:T(8,128)(2,1)S(1)}, bf16[256,512]{1,0:T(8,128)(2,1)S(1)}, u32[]{:S(2)}, u32[]{:S(2)}) collective-permute-start(bf16[256,512]{1,0:T(8,128)(2,1)S(1)} %add_convert_fusion), channel_id=1, source_target_pairs={{8,16},{16,8},{24,32},{32,24},{40,48},{48,40},{56,0},{0,56},{72,80... | collective-permute-start | bytes 786440 | tf_op jit(solution)/shard_map/ppermute | solution.py:53
  181.7 3.1 %collective-permute-start.24 = (f32[8,256]{1,0:T(8,128)S(1)}, f32[8,256]{1,0:T(8,128)S(1)}, u32[]{:S(2)}, u32[]{:S(2)}) collective-permute-start(f32[8,256]{1,0:T(8,128)S(1)} %get-tuple-element.65), channel_id=1, source_target_pairs={{0,1},{1,0},{2,3},{3,2},{4,5},{5,4},{6,7},{7,6},{8,9},{9,8},{10,11... | collective-permute-start | bytes 24584 | tf_op jit(solution)/shard_map/ppermute | solution.py:67
  184.7 5.5 %collective-permute-start.25 = (f32[8,256]{1,0:T(8,128)S(1)}, f32[8,256]{1,0:T(8,128)S(1)}, u32[]{:S(2)}, u32[]{:S(2)}) collective-permute-start(f32[8,256]{1,0:T(8,128)S(1)} %add.139.refs_1_), channel_id=1, source_target_pairs={{0,2},{1,3},{2,0},{3,1},{4,6},{5,7},{6,4},{7,5},{8,10},{9,11},{10,... | collective-permute-start | bytes 24584 | tf_op jit(solution)/shard_map/ppermute | solution.py:67
  191.2 7.0 %collective-permute-start.26 = (f32[8,256]{1,0:T(8,128)S(1)}, f32[8,256]{1,0:T(8,128)S(1)}, u32[]{:S(2)}, u32[]{:S(2)}) collective-permute-start(f32[8,256]{1,0:T(8,128)S(1)} %add.170), channel_id=1, source_target_pairs={{0,4},{1,5},{2,6},{3,7},{4,0},{5,1},{6,2},{7,3},{8,12},{9,13},{10,... | collective-permute-start | bytes 24584 | tf_op jit(solution)/shard_map/ppermute | solution.py:67
  (36 other events, 567.2 us)
Sparse Core Ops, SparseCore 0:
  10.1 53.2 all-gather.1
  122.2 47.3 reduce-scatter.1
